TPU v7x, 32 devices: a whole 2x2x4 slice. The times are simulated.
32 devices in a mesh: ctx: 8 (over z, x), ch: 2 (over y), section: 2 (over core).
Axes of the slice: x: 2, y: 2, z: 4, core: 2. Of those that a mesh axis runs over, the one named last changes fastest.
Arguments:
- mamba_x: bfloat16 [1024, 8192], P('ctx', ('ch', 'section')), may hold values from -6 to 6
- mamba_b: bfloat16 [1024, 1024], P('ctx', ('ch', 'section')), may hold values from -6 to 6
- mamba_c: bfloat16 [1024, 1024], P('ctx', ('ch', 'section')), may hold values from -6 to 6
- step_dt: float32 [1024, 64], P('ctx', ('ch', 'section')), may hold values from 0 to 0.35, as said below
- decay_a: float32 [64], P(('ch', 'section')), may hold values from 0.5 to 2
- skip_d: float32 [64], P(('ch', 'section')), may hold values from 0.5 to 1.5
- value_weight: bfloat16 [8192, 1024], P(('ch', 'section')), may hold values from -0.0625 to 0.0625
- queries: bfloat16 [1024, 8192], P('ctx', ('ch', 'section')), may hold values from -20 to 20
- keys: bfloat16 [1024, 1024], P('ctx', ('ch', 'section')), may hold values from -6 to 6
- out_grad: bfloat16 [1024, 8192], P('ctx', ('ch', 'section')), may hold values from -6 to 6
Outputs:
- attn_out: float32 [1024, 8192], P('ctx', ('ch', 'section'))
- grad_q: float32 [1024, 8192], P('ctx', ('ch', 'section'))
- grad_k: float32 [1024, 1024], P('ctx', ('ch', 'section'))
- grad_x: float32 [1024, 8192], P('ctx', ('ch', 'section'))
- grad_b: float32 [1024, 1024], P('ctx', ('ch', 'section'))
- grad_c: float32 [1024, 1024], P('ctx', ('ch', 'section'))
Inputs may be any that keep to these rules, and one draw needn't show every extreme that they name: `step_dt`: positive step sizes.
All inputs are finite; a program needn't handle non-finite values.
Results may differ from a plain program's by a relative error of at most 0.0059.
Values may be sent and summed in bfloat16 or wider, within the bound.
A program may use at most 128 MiB of HBM per device.

v0:
```python
import functools
import math

import jax
import jax.numpy as jnp
from jax import lax
from jax.sharding import PartitionSpec as P

HEAD_P = 128
STATE = 128
Q_HEADS = 64
KV_HEADS = 8
HEAD_DIM = 128


HIGHEST = lax.Precision.HIGHEST
NEG_FILL = -1e30


def carried_in(part, axis, combine, identity, reverse):
    count = lax.axis_size(axis)
    place = lax.axis_index(axis)
    ahead = count - 1 - place if reverse else place
    gathered = jax.tree.map(lambda a: lax.all_gather(a, axis), part)
    state = jax.tree.map(lambda a, e: jnp.zeros_like(a) + jnp.asarray(e, a.dtype), part, identity)

    def one(hop, state):
        source = count - 1 - hop if reverse else hop
        return combine(
            state, jax.tree.map(lambda a: lax.dynamic_index_in_dim(a, source, 0, False), gathered)
        )

    return lax.fori_loop(0, ahead, one, state)


def block_terms(inputs_x, inputs_b, inputs_c, step_sizes, decay_rates, skip_gains):
    head_count = inputs_x.shape[1]
    repeat_by = head_count // inputs_b.shape[1]
    log_sums = jnp.cumsum(-step_sizes * decay_rates[None, :], axis=0)
    positions = jnp.arange(log_sums.shape[0])
    lower_mask = (positions[:, None] >= positions[None, :])[None]
    log_gaps = log_sums.T[:, :, None] - log_sums.T[:, None, :]
    decays = jnp.where(lower_mask, jnp.exp(jnp.where(lower_mask, log_gaps, 0.0)), 0.0)
    inner_prod = jnp.einsum("tgn,sgn->gts", inputs_c, inputs_b, precision=HIGHEST)
    inner_prod = jnp.repeat(inner_prod, repeat_by, axis=0)
    mixing = inner_prod * decays * step_sizes.T[:, None, :]
    local_out = (
        jnp.einsum("hts,shp->thp", mixing, inputs_x, precision=HIGHEST)
        + skip_gains[None, :, None] * inputs_x
    )
    to_end = jnp.exp(log_sums[-1][None, :] - log_sums) * step_sizes
    b_heads = jnp.repeat(inputs_b, repeat_by, axis=1)
    weighted = inputs_x * to_end[:, :, None]
    end_state = jnp.einsum("shp,shn->hpn", weighted, b_heads, precision=HIGHEST)
    return (local_out, end_state, jnp.exp(log_sums[-1]))


def entry_terms(inputs_c, step_sizes, decay_rates, entering):
    repeat_by = entering.shape[0] // inputs_c.shape[1]
    log_sums = jnp.cumsum(-step_sizes * decay_rates[None, :], axis=0)
    c_heads = jnp.repeat(inputs_c, repeat_by, axis=1)
    carried = jnp.einsum("thn,hpn->thp", c_heads, entering, precision=HIGHEST)
    return jnp.exp(log_sums)[:, :, None] * carried


def link_states(earlier, later):
    return (earlier[0] * later[0], later[0][:, None, None] * earlier[1] + later[1])


def blockwise(carried_acc, key_piece, value_piece, update):
    segment_length = key_piece.shape[0]
    block_rows = math.gcd(segment_length, 512)

    def advance(block_index, running):
        first_row = block_index * block_rows
        key_tile_rows = lax.dynamic_slice_in_dim(key_piece, first_row, block_rows, 0)
        value_tile_rows = lax.dynamic_slice_in_dim(value_piece, first_row, block_rows, 0)
        return update(running, key_tile_rows, value_tile_rows, first_row)

    return lax.fori_loop(0, segment_length // block_rows, advance, carried_acc)


def body(
    mamba_x, mamba_b, mamba_c, step_dt, decay_a, skip_d, value_weight, queries, keys, out_grad
):
    tok_rows = mamba_x.shape[0]
    head_count = decay_a.shape[0]
    group_count = mamba_b.shape[1] // STATE
    ctx_count = lax.axis_size("ctx")
    seq_rows = tok_rows * ctx_count
    x_float = mamba_x.astype(jnp.float32).reshape(tok_rows, head_count, HEAD_P)
    b_float = mamba_b.astype(jnp.float32).reshape(tok_rows, group_count, STATE)
    readout_matrix_single = mamba_c.astype(jnp.float32).reshape(tok_rows, group_count, STATE)

    def local_part(arg_x, arg_b, arg_c):
        return block_terms(arg_x, arg_b, arg_c, step_dt, decay_a, skip_d)

    (local_out, end_state, end_decay), pull_local = jax.vjp(
        local_part, x_float, b_float, readout_matrix_single
    )
    identity = (jnp.ones_like(end_decay), jnp.zeros_like(end_state))
    entering = carried_in((end_decay, end_state), "ctx", link_states, identity, False)[1]

    def entry_part(arg_c, arg_entering):
        return entry_terms(arg_c, step_dt, decay_a, arg_entering)

    entry_out, pull_entry = jax.vjp(entry_part, readout_matrix_single, entering)
    mamba_y = (local_out + entry_out).astype(jnp.bfloat16).reshape(tok_rows, head_count * HEAD_P)
    value_terms = jnp.dot(mamba_y, value_weight, preferred_element_type=jnp.float32)
    values = lax.psum_scatter(
        value_terms, ("ch", "section"), scatter_dimension=1, tiled=True
    ).astype(jnp.bfloat16)
    kv_dev = keys.shape[1] // HEAD_DIM
    rep_count = Q_HEADS // KV_HEADS
    query_head_rows = queries.reshape(tok_rows, kv_dev, rep_count, HEAD_DIM)
    gradient_per_head = out_grad.reshape(tok_rows, kv_dev, rep_count, HEAD_DIM)
    key_heads = keys.reshape(tok_rows, kv_dev, HEAD_DIM)
    value_heads = values.reshape(tok_rows, kv_dev, HEAD_DIM)
    own_index = lax.axis_index("ctx")
    query_pos = own_index * tok_rows + jnp.arange(tok_rows)
    scale_by = 1.0 / math.sqrt(HEAD_DIM)

    def masked_scores(key_tile_rows, first_row):
        scores = (
            jnp.einsum(
                "iuan,yun->uaiy", query_head_rows, key_tile_rows, preferred_element_type=jnp.float32
            )
            * scale_by
        )
        visible = (first_row + jnp.arange(key_tile_rows.shape[0]))[None, :] <= query_pos[:, None]
        return (jnp.where(visible, scores, NEG_FILL), visible)

    def add_stats(running, key_tile_rows, value_tile_rows, first_row):
        row_top, row_total = running
        scores, visible = masked_scores(key_tile_rows, first_row)
        new_top = jnp.maximum(row_top, jnp.max(scores, axis=-1))
        block_sum = jnp.sum(jnp.where(visible, jnp.exp(scores - new_top[..., None]), 0.0), axis=-1)
        return (new_top, row_total * jnp.exp(row_top - new_top) + block_sum)

    def probs_of(stats_pair, key_tile_rows, first_row):
        scores, visible = masked_scores(key_tile_rows, first_row)
        return jnp.where(
            visible, jnp.exp(scores - stats_pair[0][..., None]) / stats_pair[1][..., None], 0.0
        )

    def add_output(stats_pair, running, key_tile_rows, value_tile_rows, first_row):
        probability_batch = probs_of(stats_pair, key_tile_rows, first_row).astype(jnp.bfloat16)
        return running + jnp.einsum(
            "vibq,qvu->bviu", probability_batch, value_tile_rows, preferred_element_type=jnp.float32
        )

    def grad_terms(stats_pair, row_delta, key_tile_rows, value_tile_rows, first_row):
        probs = probs_of(stats_pair, key_tile_rows, first_row)
        probability_batch = probs.astype(jnp.bfloat16)
        dprobs = jnp.einsum(
            "iuan,yun->uaiy", gradient_per_head, value_tile_rows, preferred_element_type=jnp.float32
        )
        score_gradient_batch = (probs * (dprobs - row_delta[..., None])).astype(jnp.bfloat16)
        query_term = jnp.einsum(
            "vibq,qvu->bviu",
            score_gradient_batch,
            key_tile_rows,
            preferred_element_type=jnp.float32,
        )
        key_term = (
            jnp.einsum(
                "xucw,cxuh->wxh",
                score_gradient_batch,
                query_head_rows,
                preferred_element_type=jnp.float32,
            )
            * scale_by
        )
        value_term = jnp.einsum(
            "xucw,cxuh->wxh",
            probability_batch,
            gradient_per_head,
            preferred_element_type=jnp.float32,
        )
        return (query_term, key_term, value_term)

    def add_grads(stats_pair, row_delta, running, key_tile_rows, value_tile_rows, first_row):
        query_acc, key_acc, value_acc = running
        query_term, key_term, value_term = grad_terms(
            stats_pair, row_delta, key_tile_rows, value_tile_rows, first_row
        )
        key_acc = lax.dynamic_update_slice_in_dim(key_acc, key_term, first_row, 0)
        value_acc = lax.dynamic_update_slice_in_dim(value_acc, value_term, first_row, 0)
        return (query_acc + query_term, key_acc, value_acc)

    stats_init = (
        jnp.full((kv_dev, rep_count, tok_rows), NEG_FILL, jnp.float32),
        jnp.zeros((kv_dev, rep_count, tok_rows), jnp.float32),
    )
    output_init = jnp.zeros((tok_rows, kv_dev, rep_count, HEAD_DIM), jnp.float32)
    piece = (
        lax.all_gather(key_heads, "ctx", axis=0, tiled=True),
        lax.all_gather(value_heads, "ctx", axis=0, tiled=True),
    )
    stats_pair = blockwise(stats_init, piece[0], piece[1], add_stats)
    piece = (
        lax.all_gather(key_heads, "ctx", axis=0, tiled=True),
        lax.all_gather(value_heads, "ctx", axis=0, tiled=True),
    )
    output_acc = blockwise(
        output_init, piece[0], piece[1], functools.partial(add_output, stats_pair)
    )
    delta_rows = jnp.sum(gradient_per_head.astype(jnp.float32) * output_acc, axis=-1)
    row_delta = delta_rows.transpose(1, 2, 0)
    grads_init = (
        jnp.zeros((tok_rows, kv_dev, rep_count, HEAD_DIM), jnp.float32),
        jnp.zeros((seq_rows, kv_dev, HEAD_DIM), jnp.float32),
        jnp.zeros((seq_rows, kv_dev, HEAD_DIM), jnp.float32),
    )
    piece = (
        lax.all_gather(key_heads, "ctx", axis=0, tiled=True),
        lax.all_gather(value_heads, "ctx", axis=0, tiled=True),
    )
    query_acc, key_acc, value_acc = blockwise(
        grads_init, piece[0], piece[1], functools.partial(add_grads, stats_pair, row_delta)
    )
    key_local, value_local = (
        lax.psum_scatter(key_acc, "ctx", scatter_dimension=0, tiled=True),
        lax.psum_scatter(value_acc, "ctx", scatter_dimension=0, tiled=True),
    )
    attn_out = output_acc.reshape(tok_rows, kv_dev * rep_count * HEAD_DIM)
    grad_q = (query_acc * scale_by).reshape(tok_rows, kv_dev * rep_count * HEAD_DIM)
    grad_k = key_local.reshape(tok_rows, kv_dev * HEAD_DIM)
    value_grad = value_local.astype(jnp.bfloat16).reshape(tok_rows, kv_dev * HEAD_DIM)
    mamba_grad = lax.dot_general(
        lax.all_gather(value_grad, ("ch", "section"), axis=1, tiled=True),
        value_weight,
        (((1,), (1,)), ((), ())),
        preferred_element_type=jnp.float32,
    )
    grad_heads_y = mamba_grad.reshape(tok_rows, head_count, HEAD_P)
    c_entry_grad, entering_grad = pull_entry(grad_heads_y)
    state_grad = carried_in((end_decay, entering_grad), "ctx", link_states, identity, True)[1]
    x_grad, b_grad, c_local_grad = pull_local((grad_heads_y, state_grad, jnp.zeros_like(end_decay)))
    grad_x = x_grad.reshape(tok_rows, head_count * HEAD_P)
    grad_b = b_grad.reshape(tok_rows, group_count * STATE)
    grad_c = (c_local_grad + c_entry_grad).reshape(tok_rows, group_count * STATE)
    return (attn_out, grad_q, grad_k, grad_x, grad_b, grad_c)


def solution(mesh):
    in_specs = (
        P("ctx", ("ch", "section")),
        P("ctx", ("ch", "section")),
        P("ctx", ("ch", "section")),
        P("ctx", ("ch", "section")),
        P(("ch", "section")),
        P(("ch", "section")),
        P(("ch", "section"), None),
        P("ctx", ("ch", "section")),
        P("ctx", ("ch", "section")),
        P("ctx", ("ch", "section")),
    )
    out_specs = (
        P("ctx", ("ch", "section")),
        P("ctx", ("ch", "section")),
        P("ctx", ("ch", "section")),
        P("ctx", ("ch", "section")),
        P("ctx", ("ch", "section")),
        P("ctx", ("ch", "section")),
    )
    return jax.shard_map(body, mesh=mesh, in_specs=in_specs, out_specs=out_specs, check_vma=False)
```

profile of v0, /device:TPU:0, one launch (start us, length us, event | category | flops | bytes accessed | tf_op | source)
XLA Modules:
  0.0 538.6 jit_solution(17368725442201988656)
XLA Ops:
  11.6 2.2 fusion.64
  14.5 31.9 %all_gather.34 = bf16[1024,2,128]{0,2,1:T(8,128)(2,1)S(1)} all-gather(bf16[128,2,128]{0,2,1:T(8,128)(2,1)S(1)} %bitcast.310), channel_id=1, replica_groups=mesh['ctx'=8,'ch'=2,'section'=2] {'ctx'}, dimensions={0}, use_global_device_ids=true | all-gather | bytes 589824 | tf_op jit(solution)/shard_map/all_gather | solution.py:202
  48.6 19.5 %all-gather.2 = f32[8,1,16]{2,1,0:T(1,128)S(1)} all-gather(f32[1,1,16]{2,1,0:T(1,128)S(1)} %get-tuple-element.843), channel_id=1, replica_groups=mesh['ctx'=8,'ch'=2,'section'=2] {'ctx'}, dimensions={0}, use_global_device_ids=true | all-gather | bytes 576 | tf_op jit(solution)/shard_map/all_gather | solution.py:24
  69.3 78.0 %all-gather.6.cloned.1.call-done = f32[128,128,128]{2,1,0:T(8,128)} async-done(((f32[16,128,128]{2,1,0:T(8,128)}), f32[128,128,128]{2,1,0:T(8,128)}) %all-gather.6.cloned.1.call-update) | async-done | bytes 8388624 | tf_op jit(solution)/shard_map/all_gather | solution.py:24
  148.5 2.3 fusion.62
  150.8 1.6 fusion.82
  152.5 14.1 %while.76 = (s32[]{:T(128)}, f32[2,8,128]{2,1,0:T(8,128)S(1)}, f32[2,8,128]{2,1,0:T(8,128)S(1)}, bf16[1024,2,128]{2,0,1:T(8,128)(2,1)}, bf16[128,2,8,128]{3,0,2,...) while((s32[]{:T(128)}, f32[2,8,128]{2,1,0:T(8,128)S(1)}, ...), condition=%wide.region_7.8_spmd.clone, body=%wide.region_4.7_spmd.clone.sunk | while | flops 276900480 | bytes 9483434 | solution.py:80
  152.7 3.6 fusion.140
  156.3 3.2 select_reduce_fusion.2
  159.7 3.6 fusion.140
  163.3 3.2 select_reduce_fusion.2
  168.9 13.8 %reduce-scatter.4.cloned.1.call-done = f32[128,256]{1,0:T(8,128)} async-done(((f32[128,1024]{1,0:T(8,128)}), f32[128,256]{1,0:T(8,128)}) %reduce-scatter.4.cloned.1.call-update) | async-done | bytes 131088 | tf_op jit(solution)/shard_map/reduce_scatter | solution.py:110
  183.7 33.6 %all_gather.33 = bf16[1024,2,128]{2,0,1:T(8,128)(2,1)} all-gather(bf16[128,2,128]{2,0,1:T(8,128)(2,1)S(1)} %copy_bitcast_fusion.1), channel_id=1, replica_groups=mesh['ctx'=8,'ch'=2,'section'=2] {'ctx'}, dimensions={0}, use_global_device_ids=true | all-gather | bytes 589824 | tf_op jit(solution)/shard_map/all_gather | solution.py:203
  217.3 5.8 %while.77 = (s32[]{:T(128)}, f32[128,2,8,128]{0,3,2,1:T(8,128)S(1)}, bf16[1024,2,128]{2,0,1:T(8,128)(2,1)}, bf16[1024,2,128]{2,0,1:T(8,128)(2,1)}, bf16[128,2,8,...) while((s32[]{:T(128)}, ...), condition=%wide.region_9.10_spmd.clone, body=%wide.region_8.9_spmd.clone.sunk | while | flops 543752832 | bytes 3300020 | solution.py:80
  217.5 2.7 fusion.145
  220.4 2.7 fusion.145
  225.5 28.6 %while.78 = (s32[]{:T(128)}, f32[128,2,8,128]{0,3,2,1:T(8,128)}, f32[1024,2,128]{2,0,1:T(8,128)}, f32[1024,2,128]{0,2,1:T(8,128)}, bf16[1024,2,128]{2,0,1:T(8,12...) while((s32[]{:T(128)}, f32[128,2,8,128]{0,3,2,1:T(8,128)}, ...), condition=%wide.region_12.13_spmd.clone, body=%wide.region_11.12_spmd.clone.sunk | while | flops 1352336000 | bytes 67007860 | solution.py:80
  225.7 2.3 fusion.156
  228.0 1.9 copy-done
  230.0 1.7 fusion.157
  231.7 2.5 fusion.159
  234.2 2.6 fusion.158
  236.8 1.8 fusion.160
  239.8 2.3 fusion.156
  242.1 1.9 copy-done
  244.1 1.7 fusion.157
  245.8 2.6 fusion.159
  248.3 2.9 fusion.158
  251.2 1.8 fusion.160
  254.7 63.5 %reduce-scatter.8.cloned.1.call-done = f32[128,2,128]{0,2,1:T(8,128)} async-done(((f32[1024,2,128]{0,2,1:T(8,128)}), f32[128,2,128]{0,2,1:T(8,128)}) %reduce-scatter.8.cloned.1.call-update) | async-done | bytes 131088 | tf_op jit(solution)/shard_map/reduce_scatter | solution.py:224
  319.1 6.0 %all_gather.35 = bf16[128,1024]{0,1:T(8,128)(2,1)S(1)} all-gather(bf16[128,256]{0,1:T(8,128)(2,1)S(1)} %bitcast.309), channel_id=1, replica_groups=mesh['ctx'=8,'ch'=2,'section'=2] {'ch','section'}, dimensions={1}, use_global_device_ids=true | all-gather | bytes 327680 | tf_op jit(solution)/shard_map/all_gather | solution.py:231
  325.1 3.5 fusion.83
  328.7 3.4 fusion.69
  333.2 2.6 copy.147
  335.8 2.5 copy.146
  338.3 1.8 bitcast_reduce_fusion
  342.5 41.5 %reduce-scatter.6.cloned.1.call-done = f32[128,2,128]{2,0,1:T(8,128)} async-done(((f32[1024,2,128]{2,0,1:T(8,128)}), f32[128,2,128]{2,0,1:T(8,128)}) %reduce-scatter.6.cloned.1.call-update) | async-done | bytes 131088 | tf_op jit(solution)/shard_map/reduce_scatter | solution.py:223
  384.0 1.6 copy_bitcast_fusion
  385.6 124.6 %all-gather.8.cloned.1.call-done = f32[128,128,128]{2,1,0:T(8,128)} async-done(((f32[16,128,128]{2,1,0:T(8,128)}), f32[128,128,128]{2,1,0:T(8,128)}) %all-gather.8.cloned.1.call-update) | async-done | bytes 8388624 | tf_op jit(solution)/shard_map/all_gather | solution.py:24
  510.4 10.6 %while.75 = (s32[]{:T(128)}, f32[16,128,128]{2,1,0:T(8,128)S(1)}, s32[]{:T(128)}, f32[8,16]{1,0:T(8,128)S(1)}, f32[8,16,128,128]{3,2,1,0:T(8,128)}, /*index=5*/s32[]{:T(128)}, s32[]{:T(128)}, s32[]{:T(128)}, s32[]{:T(128)}) while((s32[]{:T(128)}, f32[16,128,128]{2,1,0:T(8,128)S(1)}, s32[]{:T(128)}, f32[8,16]{1,0:T(8,128)S(1)}, ...), condition=%wide.region_16.17_spmd, body=%wide.region_15.16_spmd.sunk | while | flops 524294 | bytes 3146067 | solution.py:33
  510.4 1.5 bitcast_add_fusion.5
  512.0 1.4 bitcast_add_fusion.5
  513.5 1.4 bitcast_add_fusion.5
  518.0 1.4 bitcast_add_fusion.5
  519.5 1.4 bitcast_add_fusion.5
  520.9 2.9 bitcast_reduce_fusion.1
  523.8 3.3 fusion.58
  528.1 2.7 fusion.56
  (141 shorter events, 28.5 us)
Async XLA Ops:
  7.2 6.8 %copy-start.16 = (bf16[128,256]{1,0:T(8,128)(2,1)S(1)}, bf16[128,256]{1,0:T(8,128)(2,1)}, u32[]{:S(2)}) copy-start(bf16[128,256]{1,0:T(8,128)(2,1)} %param.22) | copy-start | bytes 196612
  7.2 7.2 %copy-start.17 = (bf16[128,256]{1,0:T(8,128)(2,1)S(1)}, bf16[128,256]{1,0:T(8,128)(2,1)}, u32[]{:S(2)}) copy-start(bf16[128,256]{1,0:T(8,128)(2,1)} %param.28) | copy-start | bytes 196612
  7.2 140.1 %all-gather.6.cloned.1.call-start = ((), (), s32[]{:S(2)}) async-start(), calls=%async_computation.6 | async-start | bytes 9437184 | tf_op jit(solution)/shard_map/all_gather | solution.py:24
  9.2 38.2 %copy-start.14 = (bf16[128,2048]{1,0:T(8,128)(2,1)S(1)}, bf16[128,2048]{1,0:T(8,128)(2,1)}, u32[]{:S(2)}) copy-start(bf16[128,2048]{1,0:T(8,128)(2,1)} %param.27) | copy-start | bytes 1572868
  10.6 57.5 %copy-start.11 = (bf16[128,2048]{0,1:T(8,128)(2,1)}, bf16[128,2048]{0,1:T(8,128)(2,1)S(1)}, u32[]{:S(2)}) copy-start(bf16[128,2048]{0,1:T(8,128)(2,1)S(1)} %copy.96) | copy-start | bytes 1572868
  11.6 36.6 %copy-start.8 = (f32[128,2,8,128]{3,0,2,1:T(8,128)}, f32[128,2,8,128]{3,0,2,1:T(8,128)S(1)}, u32[]{:S(2)}) copy-start(f32[128,2,8,128]{3,0,2,1:T(8,128)S(1)} %broadcast_in_dim.156) | copy-start | bytes 3145732
  11.6 36.6 %copy-start.15 = (f32[128,16]{0,1:T(8,128)S(1)}, f32[128,16]{0,1:T(8,128)}, u32[]{:S(2)}) copy-start(f32[128,16]{0,1:T(8,128)} %param.23) | copy-start | bytes 24580
  13.8 54.3 %copy-start.18 = (f32[16]{0:T(128)S(1)}, f32[16]{0:T(128)}, u32[]{:S(2)}) copy-start(f32[16]{0:T(128)} %param.25) | copy-start | bytes 196
  13.8 168.9 %reduce-scatter.4.cloned.1.call-start = ((), (), s32[]{:S(2)}) async-start(), calls=%async_computation.3 | async-start | bytes 655360 | tf_op jit(solution)/shard_map/reduce_scatter | solution.py:110
  48.6 98.7 %copy-start.10 = (f32[16,128,128]{2,1,0:T(8,128)}, f32[16,128,128]{2,1,0:T(8,128)S(1)}, u32[]{:S(2)}) copy-start(f32[16,128,128]{2,1,0:T(8,128)S(1)} %fusion.71) | copy-start | bytes 3145732
  147.4 3.4 copy-start.6
  147.6 1.0 copy-start.7
  152.4 165.8 %reduce-scatter.8.cloned.1.call-start = ((), (), s32[]{:S(2)}) async-start(), calls=%async_computation.5 | async-start | bytes 1179648 | tf_op jit(solution)/shard_map/reduce_scatter | solution.py:224
  223.1 2.4 copy-start.13
  225.5 2.5 copy-start.3
  225.7 4.3 copy-start.2
  228.0 2.0 copy-start
  234.2 2.6 copy-start.1
  236.8 2.9 copy-start.4
  239.6 2.5 copy-start.3
  239.8 4.3 copy-start.2
  242.1 2.0 copy-start
  248.3 2.9 copy-start.1
  251.2 2.9 copy-start.4
  254.1 129.9 %reduce-scatter.6.cloned.1.call-start = ((), (), s32[]{:S(2)}) async-start(), calls=%async_computation.4 | async-start | bytes 1179648 | tf_op jit(solution)/shard_map/reduce_scatter | solution.py:223
  254.7 255.6 %all-gather.8.cloned.1.call-start = ((), (), s32[]{:S(2)}) async-start(), calls=%async_computation.7 | async-start | bytes 9437184 | tf_op jit(solution)/shard_map/all_gather | solution.py:24
  325.1 7.0 %copy-start.5 = (f32[128,2,8,128]{0,3,2,1:T(8,128)S(1)}, f32[128,2,8,128]{0,3,2,1:T(8,128)}, u32[]{:S(2)}) copy-start(f32[128,2,8,128]{0,3,2,1:T(8,128)} %get-tuple-element.588) | copy-start | bytes 3145732
  333.2 7.1 %copy-start.12 = (bf16[128,2048]{0,1:T(8,128)(2,1)S(1)}, bf16[128,2048]{0,1:T(8,128)(2,1)}, u32[]{:S(2)}) copy-start(bf16[128,2048]{0,1:T(8,128)(2,1)} %copy-done.11) | copy-start | bytes 1572868
  510.4 13.5 %copy-start.9 = (f32[128,2,8,128]{3,0,2,1:T(8,128)S(1)}, f32[128,2,8,128]{3,0,2,1:T(8,128)}, u32[]{:S(2)}) copy-start(f32[128,2,8,128]{3,0,2,1:T(8,128)} %copy-done.8) | copy-start | bytes 3145732
Sparse Core Ops, SparseCore 0:
  13.9 133.3 all-gather.5
  152.5 30.1 reduce-scatter.3
  254.2 63.9 reduce-scatter.7
  321.5 62.5 reduce-scatter.5
  386.2 123.9 all-gather.7
where the time goes:
time: 540 us; the launch traced here: 539 us
  waiting for transfers between devices  322 us (60%)
  blocking collectives  91.1 us (17%)
  matrix products  61.6 us (11%)
  local copies, waits for them, and re-layouts  27 us (5%)
  other arithmetic  21.8 us (4%)
  between operations  14.2 us (3%)
    all_gather x2, waiting for transfers between devices, carried_in(): gathered = jax.tree.map(lambda a: lax.all_gather(a, axis), part)  203 us
    reduce_scatter x1, waiting for transfers between devices, body(): lax.psum_scatter(value_acc, 'ctx', scatter_dimension=0, tiled=True)  63.5 us
    reduce_scatter x1, waiting for transfers between devices, body(): lax.psum_scatter(key_acc, 'ctx', scatter_dimension=0, tiled=True)  41.5 us
    all_gather x1, blocking collectives, body(): lax.all_gather(value_heads, 'ctx', axis=0, tiled=True)  33.6 us
    all_gather x1, blocking collectives, body(): lax.all_gather(key_heads, 'ctx', axis=0, tiled=True)  31.9 us
    all_gather x1, blocking collectives, carried_in(): gathered = jax.tree.map(lambda a: lax.all_gather(a, axis), part)  19.5 us
    reduce_scatter x1, waiting for transfers between devices, body(): lax.psum_scatter(value_terms, ('ch', 'section'), scatter_dimension=1, til...  13.8 us
    dot_general x4, matrix products, masked_scores(): jnp.einsum('iuan,yun->uaiy', query_head_rows, key_tile_rows, preferred_el...  11.9 us
  transfers between devices with their start and end apart: 5, of which 5 were waited for; matrix products, arithmetic and copies ran while one was open for 7% of the time, Pallas kernels for 0%

commit v1 on v0

v1 whole, which is shorter than its diff:
```python
import functools
import math

import jax
import jax.numpy as jnp
from jax import lax
from jax.experimental import pallas as pl
from jax.experimental.pallas import tpu as pltpu
from jax.sharding import PartitionSpec as P

LANE = 128
Q_HEADS = 64
KV_HEADS = 8
REP = Q_HEADS // KV_HEADS
NEG_FILL = -1e30
F32 = jnp.float32
BF16 = jnp.bfloat16
MESH = pl.DeviceIdType.MESH
VMEM_BYTES = 56 * 1024 * 1024


def nn(a, b):
    return lax.dot_general(a, b, (((1,), (0,)), ((), ())), preferred_element_type=F32)


def nt(a, b):
    return lax.dot_general(a, b, (((1,), (1,)), ((), ())), preferred_element_type=F32)


def flip(a):
    return a.astype(F32).T.astype(BF16)


def rounded(a):
    return a.astype(BF16)


def ctx_peer(me, hop, count):
    return lax.rem(me + hop, count)


def group_place(sizes):
    return lax.axis_index("ch") * sizes[1] + lax.axis_index("section")


def group_id(place, sizes):
    return {"ch": place // sizes[1], "section": lax.rem(place, sizes[1])}


def enter(ctx_count, sizes):
    me = lax.axis_index("ctx")
    mine = group_place(sizes)
    members = sizes[0] * sizes[1]
    barrier = pltpu.get_barrier_semaphore()
    for hop in range(1, ctx_count):
        pl.semaphore_signal(
            barrier, inc=1, device_id={"ctx": ctx_peer(me, hop, ctx_count)}, device_id_type=MESH
        )
    for hop in range(1, members):
        pl.semaphore_signal(
            barrier,
            inc=1,
            device_id=group_id(lax.rem(mine + hop, members), sizes),
            device_id_type=MESH,
        )
    pl.semaphore_wait(barrier, ctx_count + members - 2)


def enter_ctx(ctx_count):
    me = lax.axis_index("ctx")
    barrier = pltpu.get_barrier_semaphore()
    for hop in range(1, ctx_count):
        pl.semaphore_signal(
            barrier, inc=1, device_id={"ctx": ctx_peer(me, hop, ctx_count)}, device_id_type=MESH
        )
    pl.semaphore_wait(barrier, ctx_count - 1)


def remote(src, dst, send, recv, device):
    return pltpu.make_async_remote_copy(
        src_ref=src, dst_ref=dst, send_sem=send, recv_sem=recv, device_id=device, device_id_type=MESH
    )


def triangle(rows, lower):
    first = lax.broadcasted_iota(jnp.int32, (rows, rows), 0)
    second = lax.broadcasted_iota(jnp.int32, (rows, rows), 1)
    return first >= second if lower else second >= first


def scan_parts(me, rows):
    width = min(rows, LANE)
    for part in range(rows // width):
        yield slice(part * width, (part + 1) * width), (me * rows + part * width) // LANE


def forward_kernel(
    ctx_count, sizes,
    x_ref, b_ref, c_ref, cum_ref, cumt_ref, dt_ref, dtt_ref, skip_ref, dec_ref, w_ref, k_ref,
    kall_out, vall_out, ent_out, decall_out,
    kall, vall, decall, st_send, st_recv, en_send, en_recv, y_acc, y_b, vp_send, vp_recv,
    st_s, st_r, en_s, en_r, k_s, k_r, v_s, v_r, d_s, d_r, p_s, p_r,
):
    me = lax.axis_index("ctx")
    mine = group_place(sizes)
    members = sizes[0] * sizes[1]
    tok = x_ref.shape[0]
    heads = x_ref.shape[1] // LANE
    per_group = heads // (b_ref.shape[1] // LANE)
    rows = heads * LANE // ctx_count
    kall[...] = jnp.zeros_like(kall)
    vall[...] = jnp.zeros_like(vall)
    enter(ctx_count, sizes)
    decall[me] = dec_ref[...]
    kall[me] = k_ref[...]
    for head in range(heads):
        group = head // per_group
        if head % per_group == 0:
            b_flip = flip(b_ref[:, group * LANE:(group + 1) * LANE])
        cum = cum_ref[:, head:head + 1]
        weight = jnp.exp(cum[tok - 1:tok, :] - cum) * dt_ref[:, head:head + 1]
        xw = x_ref[:, head * LANE:(head + 1) * LANE].astype(F32) * weight
        st_send[head * LANE:(head + 1) * LANE, :] = rounded(nn(b_flip, rounded(xw)))
    sends = []
    for hop in range(1, ctx_count):
        peer = ctx_peer(me, hop, ctx_count)
        to = {"ctx": peer}
        copy = remote(decall.at[me], decall.at[me], d_s.at[hop], d_r.at[hop], to)
        copy.start()
        sends.append(copy)
        block = pl.ds(pl.multiple_of(peer * rows, 16), rows)
        copy = remote(st_send.at[block], st_recv.at[me], st_s.at[hop], st_r.at[hop], to)
        copy.start()
        sends.append(copy)
    for hop in range(1, ctx_count):
        peer = ctx_peer(me, hop, ctx_count)

        @pl.when(peer > me)
        def _():
            remote(kall.at[me], kall.at[me], k_s.at[hop], k_r.at[hop], {"ctx": peer}).start()

    st_recv[me] = st_send[pl.ds(pl.multiple_of(me * rows, 16), rows), :]
    lower = triangle(tok, True)
    for head in range(heads):
        group = head // per_group
        if head % per_group == 0:
            columns = slice(group * LANE, (group + 1) * LANE)
            inner = nt(c_ref[:, columns], b_ref[:, columns])
        gap = cum_ref[:, head:head + 1] - cumt_ref[head:head + 1, :]
        decays = jnp.where(lower, jnp.exp(jnp.where(lower, gap, 0.0)), 0.0)
        mixing = inner * decays * dtt_ref[head:head + 1, :]
        high = rounded(mixing)
        low = rounded(mixing - high.astype(F32))
        x_head = x_ref[:, head * LANE:(head + 1) * LANE]
        y_acc[:, head * LANE:(head + 1) * LANE] = (
            nn(high, x_head) + nn(low, x_head) + skip_ref[:, head:head + 1] * x_head.astype(F32)
        )
    for hop in range(1, ctx_count):
        peer = ctx_peer(me, ctx_count - hop, ctx_count)
        to = {"ctx": peer}
        remote(decall.at[me], decall.at[peer], d_s.at[hop], d_r.at[hop], to).wait_recv()
        remote(
            st_send.at[pl.ds(0, rows)], st_recv.at[peer], st_s.at[hop], st_r.at[hop], to
        ).wait_recv()
    running = [jnp.zeros((part.stop - part.start, LANE), F32) for part, _ in scan_parts(me, rows)]
    for block in range(ctx_count):
        for at, (part, head) in enumerate(scan_parts(me, rows)):
            en_send[block, part, :] = rounded(running[at])
            running[at] = (
                decall[block, pl.ds(head, 1), :] * running[at] + st_recv[block, part, :].astype(F32)
            )
    own_rows = pl.ds(pl.multiple_of(me * rows, 16), rows)
    for hop in range(1, ctx_count):
        peer = ctx_peer(me, hop, ctx_count)
        copy = remote(
            en_send.at[peer], en_recv.at[own_rows], en_s.at[hop], en_r.at[hop], {"ctx": peer}
        )
        copy.start()
        sends.append(copy)
    en_recv[own_rows, :] = en_send[me]
    for hop in range(1, ctx_count):
        peer = ctx_peer(me, ctx_count - hop, ctx_count)
        block = pl.ds(pl.multiple_of(peer * rows, 16), rows)
        remote(
            en_send.at[0], en_recv.at[block], en_s.at[hop], en_r.at[hop], {"ctx": peer}
        ).wait_recv()
    for head in range(heads):
        group = head // per_group
        span = slice(head * LANE, (head + 1) * LANE)
        carried = nn(c_ref[:, group * LANE:(group + 1) * LANE], en_recv[span, :])
        y_b[:, span] = rounded(y_acc[:, span] + jnp.exp(cum_ref[:, head:head + 1]) * carried)
    kv = k_ref.shape[1]
    for hop in list(range(1, members)) + [0]:
        place = lax.rem(mine + hop, members)
        piece = nn(y_b[...], w_ref[:, pl.ds(pl.multiple_of(place * kv, LANE), kv)])
        if hop:
            vp_send[hop] = rounded(piece)
            copy = remote(
                vp_send.at[hop], vp_recv.at[hop], p_s.at[hop], p_r.at[hop], group_id(place, sizes)
            )
            copy.start()
            sends.append(copy)
    for hop in range(1, members):
        place = lax.rem(mine + hop, members)
        remote(
            vp_send.at[hop], vp_recv.at[hop], p_s.at[hop], p_r.at[hop], group_id(place, sizes)
        ).wait_recv()
        piece = piece + vp_recv[hop].astype(F32)
    vall[me] = rounded(piece)
    for hop in range(1, ctx_count):
        peer = ctx_peer(me, hop, ctx_count)

        @pl.when(peer > me)
        def _():
            remote(vall.at[me], vall.at[me], v_s.at[hop], v_r.at[hop], {"ctx": peer}).start()

    for hop in range(1, ctx_count):
        source = ctx_peer(me, ctx_count - hop, ctx_count)

        @pl.when(source < me)
        def _():
            to = {"ctx": source}
            remote(kall.at[me], kall.at[source], k_s.at[hop], k_r.at[hop], to).wait_recv()
            remote(vall.at[me], vall.at[source], v_s.at[hop], v_r.at[hop], to).wait_recv()

    kall_out[...] = kall[...]
    vall_out[...] = vall[...]
    ent_out[...] = en_recv[...]
    decall_out[...] = decall[...]
    for copy in sends:
        copy.wait_send()
    for hop in range(1, ctx_count):
        peer = ctx_peer(me, hop, ctx_count)

        @pl.when(peer > me)
        def _():
            to = {"ctx": peer}
            remote(kall.at[me], kall.at[me], k_s.at[hop], k_r.at[hop], to).wait_send()
            remote(vall.at[me], vall.at[me], v_s.at[hop], v_r.at[hop], to).wait_send()


def attention_kernel(
    ctx_count, sizes,
    q_ref, do_ref, kall_ref, vall_ref,
    o_ref, dq_ref, dk_ref, vg_out,
    k_flip, v_flip, s_buf, dp_buf, dk_acc, dv_acc, g_send, g_recv, vg_all,
    g_s, g_r, vg_s, vg_r,
):
    me = lax.axis_index("ctx")
    mine = group_place(sizes)
    members = sizes[0] * sizes[1]
    tok = q_ref.shape[0]
    seq = kall_ref.shape[0]
    kv_dev = kall_ref.shape[1] // LANE
    chunk = math.gcd(seq, 256)
    chunks = (me * tok + tok - 1) // chunk + 1
    scale_by = 1.0 / math.sqrt(LANE)
    pair = 2 * LANE
    cols = 2 * tok
    g_recv[...] = jnp.zeros_like(g_recv)
    dk_acc[...] = jnp.zeros_like(dk_acc)
    dv_acc[...] = jnp.zeros_like(dv_acc)
    enter(ctx_count, sizes)
    query_pos = me * tok + lax.rem(lax.broadcasted_iota(jnp.int32, (chunk, cols), 1), tok)
    key_pos = lax.broadcasted_iota(jnp.int32, (chunk, cols), 0)

    for kv in range(kv_dev):
        span = slice(kv * LANE, (kv + 1) * LANE)

        def flip_chunk(at, carry):
            here = pl.ds(pl.multiple_of(at * chunk, LANE), chunk)
            k_flip[:, here] = flip(kall_ref[here, span])
            v_flip[:, here] = flip(vall_ref[here, span])
            return carry

        lax.fori_loop(0, chunks, flip_chunk, 0)

        def one_pair(index, carry):
            first = pl.multiple_of(kv * REP * LANE + index * pair, pair)
            second = pl.multiple_of(first + LANE, LANE)
            q = jnp.concatenate([q_ref[:, pl.ds(first, LANE)], q_ref[:, pl.ds(second, LANE)]], axis=0)
            do = jnp.concatenate(
                [do_ref[:, pl.ds(first, LANE)], do_ref[:, pl.ds(second, LANE)]], axis=0
            )
            q_t = flip(q)
            do_f = do.astype(F32).T
            do_t = do_f.astype(BF16)

            def scores(at, top):
                here = pl.ds(pl.multiple_of(at * chunk, LANE), chunk)
                s = nn(kall_ref[here, span], q_t) * scale_by
                s = jnp.where(key_pos + at * chunk <= query_pos, s, NEG_FILL)
                s_buf[here, :] = s
                return jnp.maximum(top, jnp.max(s, axis=0, keepdims=True))

            top = lax.fori_loop(0, chunks, scores, jnp.full((1, cols), NEG_FILL, F32))

            def totals(at, total):
                here = pl.ds(pl.multiple_of(at * chunk, LANE), chunk)
                e = jnp.exp(s_buf[here, :] - top)
                s_buf[here, :] = e
                dp_buf[here, :] = nn(vall_ref[here, span], do_t)
                return total + jnp.sum(e, axis=0, keepdims=True)

            total = lax.fori_loop(0, chunks, totals, jnp.zeros((1, cols), F32))
            inverse = 1.0 / total

            def outputs(at, o_t):
                here = pl.ds(pl.multiple_of(at * chunk, LANE), chunk)
                p = s_buf[here, :] * inverse
                s_buf[here, :] = p
                p_b = rounded(p)
                dv_acc[here, span] += nn(p_b, do)
                return o_t + nn(v_flip[:, here], p_b)

            o_t = lax.fori_loop(0, chunks, outputs, jnp.zeros((LANE, cols), F32))
            delta = jnp.sum(o_t * do_f, axis=0, keepdims=True)

            def grads(at, dq_t):
                here = pl.ds(pl.multiple_of(at * chunk, LANE), chunk)
                ds = rounded(s_buf[here, :] * (dp_buf[here, :] - delta))
                dk_acc[here, span] += nn(ds, q)
                return dq_t + nn(k_flip[:, here], ds)

            dq_t = lax.fori_loop(0, chunks, grads, jnp.zeros((LANE, cols), F32)) * scale_by
            o_ref[:, pl.ds(first, LANE)] = o_t[:, :tok].T
            o_ref[:, pl.ds(second, LANE)] = o_t[:, tok:].T
            dq_ref[:, pl.ds(first, LANE)] = dq_t[:, :tok].T
            dq_ref[:, pl.ds(second, LANE)] = dq_t[:, tok:].T
            return carry

        lax.fori_loop(0, REP // 2, one_pair, 0)
        for hop in range(1, ctx_count):
            peer = ctx_peer(me, hop, ctx_count)

            @pl.when(peer < me)
            def _():
                block = pl.ds(pl.multiple_of(peer * tok, tok), tok)
                g_send[kv, hop, 0] = rounded(dk_acc[block, span])
                g_send[kv, hop, 1] = rounded(dv_acc[block, span])
                remote(
                    g_send.at[kv, hop], g_recv.at[kv, hop], g_s.at[kv, hop], g_r.at[kv, hop],
                    {"ctx": peer},
                ).start()

    own = pl.ds(pl.multiple_of(me * tok, tok), tok)
    for kv in range(kv_dev):
        span = slice(kv * LANE, (kv + 1) * LANE)
        dk = dk_acc[own, span]
        dv = dv_acc[own, span]
        for hop in range(1, ctx_count):
            source = ctx_peer(me, ctx_count - hop, ctx_count)

            @pl.when(source > me)
            def _():
                remote(
                    g_send.at[kv, hop], g_recv.at[kv, hop], g_s.at[kv, hop], g_r.at[kv, hop],
                    {"ctx": source},
                ).wait_recv()

            dk = dk + g_recv[kv, hop, 0].astype(F32)
            dv = dv + g_recv[kv, hop, 1].astype(F32)
        dk_ref[:, span] = dk * scale_by
        vg_all[mine, :, span] = rounded(dv)
    sends = []
    for hop in range(1, members):
        place = lax.rem(mine + hop, members)
        copy = remote(
            vg_all.at[mine], vg_all.at[mine], vg_s.at[hop], vg_r.at[hop], group_id(place, sizes)
        )
        copy.start()
        sends.append(copy)
    for hop in range(1, members):
        place = lax.rem(mine + members - hop, members)
        remote(
            vg_all.at[mine], vg_all.at[place], vg_s.at[hop], vg_r.at[hop], group_id(place, sizes)
        ).wait_recv()
    vg_out[...] = vg_all[...]
    for copy in sends:
        copy.wait_send()
    for kv in range(kv_dev):
        for hop in range(1, ctx_count):
            peer = ctx_peer(me, hop, ctx_count)

            @pl.when(peer < me)
            def _():
                remote(
                    g_send.at[kv, hop], g_recv.at[kv, hop], g_s.at[kv, hop], g_r.at[kv, hop],
                    {"ctx": peer},
                ).wait_send()


def backward_kernel(
    ctx_count,
    x_ref, b_ref, c_ref, cum_ref, cumt_ref, dt_ref, dtt_ref, skip_ref, w_ref, ent_ref, decall, vg_ref,
    dx_ref, db_ref, dc_ref,
    g_acc, st_send, st_recv, en_send, en_recv,
    st_s, st_r, en_s, en_r,
):
    me = lax.axis_index("ctx")
    tok = x_ref.shape[0]
    heads = x_ref.shape[1] // LANE
    groups = b_ref.shape[1] // LANE
    per_group = heads // groups
    rows = heads * LANE // ctx_count
    kv = vg_ref.shape[2]
    enter_ctx(ctx_count)
    for group in range(groups):
        wide = slice(group * per_group * LANE, (group + 1) * per_group * LANE)
        total = None
        for place in range(vg_ref.shape[0]):
            term = nt(vg_ref[place], w_ref[wide, place * kv:(place + 1) * kv])
            total = term if total is None else total + term
        g_acc[:, wide] = total
        c_flip = flip(c_ref[:, group * LANE:(group + 1) * LANE])
        for head in range(group * per_group, (group + 1) * per_group):
            span = slice(head * LANE, (head + 1) * LANE)
            scaled = rounded(jnp.exp(cum_ref[:, head:head + 1]) * g_acc[:, span])
            st_send[span, :] = rounded(nn(c_flip, scaled))
    sends = []
    for hop in range(1, ctx_count):
        peer = ctx_peer(me, hop, ctx_count)
        block = pl.ds(pl.multiple_of(peer * rows, 16), rows)
        copy = remote(st_send.at[block], st_recv.at[me], st_s.at[hop], st_r.at[hop], {"ctx": peer})
        copy.start()
        sends.append(copy)
    own_rows = pl.ds(pl.multiple_of(me * rows, 16), rows)
    st_recv[me] = st_send[own_rows, :]
    lower = triangle(tok, True)
    upper = triangle(tok, False)
    for group in range(groups):
        columns = slice(group * LANE, (group + 1) * LANE)
        b = b_ref[:, columns]
        c = c_ref[:, columns]
        inner_t = nt(b, c)
        inner_grad = jnp.zeros((tok, tok), F32)
        dc = jnp.zeros((tok, LANE), F32)
        for head in range(group * per_group, (group + 1) * per_group):
            span = slice(head * LANE, (head + 1) * LANE)
            cum = cum_ref[:, head:head + 1]
            cum_t = cumt_ref[head:head + 1, :]
            decays = jnp.where(lower, jnp.exp(jnp.where(lower, cum - cum_t, 0.0)), 0.0)
            decays_t = jnp.where(upper, jnp.exp(jnp.where(upper, cum_t - cum, 0.0)), 0.0)
            mixing_t = rounded(inner_t * decays_t * dt_ref[:, head:head + 1])
            g = g_acc[:, span]
            g_b = rounded(g)
            dx_ref[:, span] = nn(mixing_t, g_b) + skip_ref[:, head:head + 1] * g
            inner_grad = inner_grad + nt(g_b, x_ref[:, span]) * decays * dtt_ref[head:head + 1, :]
            dc = dc + nt(rounded(jnp.exp(cum) * g), ent_ref[span, :])
        dc_ref[:, columns] = dc + nn(rounded(inner_grad), b)
        db_ref[:, columns] = nn(rounded(inner_grad.T), c)
    for hop in range(1, ctx_count):
        peer = ctx_peer(me, ctx_count - hop, ctx_count)
        remote(
            st_send.at[pl.ds(0, rows)], st_recv.at[peer], st_s.at[hop], st_r.at[hop], {"ctx": peer}
        ).wait_recv()
    running = [jnp.zeros((part.stop - part.start, LANE), F32) for part, _ in scan_parts(me, rows)]
    for block in range(ctx_count - 1, -1, -1):
        for at, (part, head) in enumerate(scan_parts(me, rows)):
            en_send[block, part, :] = rounded(running[at])
            running[at] = (
                decall[block, pl.ds(head, 1), :] * running[at] + st_recv[block, part, :].astype(F32)
            )
    for hop in range(1, ctx_count):
        peer = ctx_peer(me, hop, ctx_count)
        copy = remote(
            en_send.at[peer], en_recv.at[own_rows], en_s.at[hop], en_r.at[hop], {"ctx": peer}
        )
        copy.start()
        sends.append(copy)
    en_recv[own_rows, :] = en_send[me]
    for hop in range(1, ctx_count):
        peer = ctx_peer(me, ctx_count - hop, ctx_count)
        block = pl.ds(pl.multiple_of(peer * rows, 16), rows)
        remote(
            en_send.at[0], en_recv.at[block], en_s.at[hop], en_r.at[hop], {"ctx": peer}
        ).wait_recv()
    for group in range(groups):
        columns = slice(group * LANE, (group + 1) * LANE)
        b = b_ref[:, columns]
        db = db_ref[:, columns]
        for head in range(group * per_group, (group + 1) * per_group):
            span = slice(head * LANE, (head + 1) * LANE)
            cum = cum_ref[:, head:head + 1]
            weight = jnp.exp(cum[tok - 1:tok, :] - cum) * dt_ref[:, head:head + 1]
            dstate = en_recv[span, :]
            dx_ref[:, span] += weight * nn(b, dstate)
            db = db + nt(rounded(x_ref[:, span].astype(F32) * weight), dstate)
        db_ref[:, columns] = db
    for copy in sends:
        copy.wait_send()


def body(
    sizes,
    mamba_x, mamba_b, mamba_c, step_dt, decay_a, skip_d, value_weight, queries, keys, out_grad
):
    tok = mamba_x.shape[0]
    heads = decay_a.shape[0]
    n = lax.axis_size("ctx")
    members = sizes[0] * sizes[1]
    kv = keys.shape[1]
    kv_dev = kv // LANE
    seq = n * tok
    rows = heads * LANE // n
    cum = jnp.cumsum(-step_dt * decay_a[None, :], axis=0)
    cum_t = cum.T
    dt_t = step_dt.T
    skip = skip_d[None, :]
    decay = jnp.broadcast_to(jnp.exp(cum[-1])[:, None], (heads, LANE))
    vmem = pl.BlockSpec(memory_space=pltpu.VMEM)
    dma = pltpu.SemaphoreType.DMA

    def call(kernel, operands, outs, scratch, ident):
        return pl.pallas_call(
            kernel,
            out_shape=[jax.ShapeDtypeStruct(shape, kind) for shape, kind in outs],
            in_specs=[vmem] * len(operands),
            out_specs=[vmem] * len(outs),
            scratch_shapes=scratch,
            compiler_params=pltpu.CompilerParams(
                collective_id=ident, has_side_effects=True, vmem_limit_bytes=VMEM_BYTES
            ),
        )(*operands)

    kall, vall, ent, decall = call(
        functools.partial(forward_kernel, n, sizes),
        (mamba_x, mamba_b, mamba_c, cum, cum_t, step_dt, dt_t, skip, decay, value_weight, keys),
        [((n, tok, kv), BF16), ((n, tok, kv), BF16), ((heads * LANE, LANE), BF16),
         ((n, heads, LANE), F32)],
        [
            pltpu.VMEM((n, tok, kv), BF16),
            pltpu.VMEM((n, tok, kv), BF16),
            pltpu.VMEM((n, heads, LANE), F32),
            pltpu.VMEM((heads * LANE, LANE), BF16),
            pltpu.VMEM((n, rows, LANE), BF16),
            pltpu.VMEM((n, rows, LANE), BF16),
            pltpu.VMEM((heads * LANE, LANE), BF16),
            pltpu.VMEM((tok, heads * LANE), F32),
            pltpu.VMEM((tok, heads * LANE), BF16),
            pltpu.VMEM((members, tok, kv), BF16),
            pltpu.VMEM((members, tok, kv), BF16),
        ] + [dma((n,))] * 10 + [dma((members,))] * 2,
        0,
    )
    attn_out, grad_q, grad_k, vg = call(
        functools.partial(attention_kernel, n, sizes),
        (queries, out_grad, kall.reshape(seq, kv), vall.reshape(seq, kv)),
        [(queries.shape, F32), (queries.shape, F32), (keys.shape, F32), ((members, tok, kv), BF16)],
        [
            pltpu.VMEM((LANE, seq), BF16),
            pltpu.VMEM((LANE, seq), BF16),
            pltpu.VMEM((seq, 2 * tok), F32),
            pltpu.VMEM((seq, 2 * tok), F32),
            pltpu.VMEM((seq, kv), F32),
            pltpu.VMEM((seq, kv), F32),
            pltpu.VMEM((kv_dev, n, 2, tok, LANE), BF16),
            pltpu.VMEM((kv_dev, n, 2, tok, LANE), BF16),
            pltpu.VMEM((members, tok, kv), BF16),
            dma((kv_dev, n)), dma((kv_dev, n)), dma((members,)), dma((members,)),
        ],
        1,
    )
    grad_x, grad_b, grad_c = call(
        functools.partial(backward_kernel, n),
        (mamba_x, mamba_b, mamba_c, cum, cum_t, step_dt, dt_t, skip, value_weight, ent, decall, vg),
        [(mamba_x.shape, F32), (mamba_b.shape, F32), (mamba_c.shape, F32)],
        [
            pltpu.VMEM((tok, heads * LANE), F32),
            pltpu.VMEM((heads * LANE, LANE), BF16),
            pltpu.VMEM((n, rows, LANE), BF16),
            pltpu.VMEM((n, rows, LANE), BF16),
            pltpu.VMEM((heads * LANE, LANE), BF16),
        ] + [dma((n,))] * 4,
        2,
    )
    return (attn_out, grad_q, grad_k, grad_x, grad_b, grad_c)


def solution(mesh):
    split = P("ctx", ("ch", "section"))
    per_head = P(("ch", "section"))
    in_specs = (
        split, split, split, split, per_head, per_head, P(("ch", "section"), None), split, split, split
    )
    sizes = (mesh.shape["ch"], mesh.shape["section"])
    return jax.shard_map(
        functools.partial(body, sizes),
        mesh=mesh, in_specs=in_specs, out_specs=(split,) * 6, check_vma=False,
    )
```

time: 540 us -> 151 us (0.28)
  waiting for transfers between devices: 322 us -> 0 us
  Pallas kernels: 0 us -> 139 us
  blocking collectives: 91.1 us -> 0 us
  matrix products: 61.6 us -> 0 us
  other arithmetic: 21.8 us -> 0.94 us
  local copies, waits for them, and re-layouts: 27 us -> 7.78 us
  between operations: 14.2 us -> 0.73 us
    all_gather x2 -> x0, waiting for transfers between devices: 203 us -> none  [carried_in(): gathered = jax.tree.map(lambda a: lax.all_gather(a, axis), part)]
    pallas_call x0 -> x3, Pallas kernels: none -> 139 us  [call(): pl.pallas_call(kernel, out_shape=[jax.ShapeDtypeStruct(shape, kind) for s...]
    reduce_scatter x3 -> x0, waiting for transfers between devices: 119 us -> none  [the longest x1 63.5 us: body(): lax.psum_scatter(value_acc, 'ctx', scatter_dimension=0, tiled=True)]
    all_gather x4 -> x0, blocking collectives: 91.1 us -> none  [the longest x1 33.6 us: body(): lax.all_gather(value_heads, 'ctx', axis=0, tiled=True)]
    dot_general x28 -> x0, matrix products: 61.6 us -> none  [the longest x4 11.9 us: masked_scores(): jnp.einsum('iuan,yun->uaiy', query_head_rows, key_tile_rows, preferred_el...]
    add x21 -> x0, other arithmetic: 10.3 us -> none  [the longest x7 10.2 us: link_states(): later[0][:, None, None] * earlier[1] + later[1]]
    reshape x9 -> x0, local copies, waits for them, and re-layouts: 7.9 us -> none  [the longest x1 2.59 us: body(): (query_acc * scale_by).reshape(tok_rows, kv_dev * rep_count * HEAD_DIM)]
    reduce_sum x3 -> x0, other arithmetic: 6.49 us -> none  [the longest x2 6.36 us: add_stats(): jnp.sum(jnp.where(visible, jnp.exp(scores - new_top[..., None]), 0.0), ax...]
  transfers between devices with their start and end apart: 5 -> 0, of which waited for: 5 -> 0; matrix products, arithmetic and copies ran while one was open for 7% -> 0% of each run, Pallas kernels for 0% -> 0%
where the time goes in v1:
time: 151 us; the launch traced here: 148 us
  Pallas kernels  139 us (92%)
  local copies, waits for them, and re-layouts  7.78 us (5%)
    pallas_call x3, Pallas kernels, call(): pl.pallas_call(kernel, out_shape=[jax.ShapeDtypeStruct(shape, kind) for s...  139 us
    unnamed x21, local copies, waits for them, and re-layouts  6.33 us

profile of v1, /device:TPU:0, one launch (start us, length us, event | category | flops | bytes accessed | tf_op | source)
XLA Modules:
  0.0 148.3 jit_solution(14650234876197351044)
XLA Ops:
  0.6 0.8 negate_multiply_fusion
  1.4 0.1 copy.16
  1.5 0.2 reduce_window_sum.11.cum_ref
  1.7 0.0 copy-start
  1.7 0.7 broadcast_in_dim.5.dec_ref
  2.4 0.7 copy.17
  3.0 1.4 copy.18.dt_ref
  4.5 0.0 copy-done
  4.5 50.9 %shard_map.145 = (bf16[8,128,256]{2,1,0:T(8,128)(2,1)}, bf16[8,128,256]{2,1,0:T(8,128)(2,1)}, bf16[2048,128]{1,0:T(8,128)(2,1)}, f32[8,16,128]{2,1,0:T(8,128)}) custom-call(bf16[128,2048]{1,0:T(8,128)(2,1)} %x_ref.3, bf16[128,256]{1,0:T(8,128)(2,1)} %b_ref.3, bf16[128,256]{1,0:T(8,128)(2,1)} %c_ref.3, f32[128,16]{1,0:T(8,128)} %copy-done, ...), custom_call_target="tpu_custom_call" | custom-call | tf_op jit(solution)/shard_map/pallas_call | solution.py:515
  55.3 52.7 %shard_map.146 = (f32[128,2048]{1,0:T(8,128)}, f32[128,2048]{1,0:T(8,128)}, f32[128,256]{1,0:T(8,128)}, bf16[4,128,256]{2,1,0:T(8,128)(2,1)}) custom-call(bf16[128,2048]{1,0:T(8,128)(2,1)} %q_ref.1, bf16[128,2048]{1,0:T(8,128)(2,1)} %do_ref.1, bf16[1024,256]{1,0:T(8,128)(2,1)} %bitcast.7, bf16[1024,256]{1,0:T(8,128)(2,1)} %bitcast.8), custom_call_target="tpu_custom_call" | custom-call | tf_op jit(solution)/shard_map/pallas_call | solution.py:515
  108.1 0.0 copy-start.2
  108.1 0.0 copy-start.1
  108.1 0.0 copy-start.4
  108.1 35.2 %shard_map.147 = (f32[128,2048]{1,0:T(8,128)}, f32[128,256]{1,0:T(8,128)}, f32[128,256]{1,0:T(8,128)}) custom-call(bf16[128,2048]{1,0:T(8,128)(2,1)} %x_ref.3, bf16[128,256]{1,0:T(8,128)(2,1)} %b_ref.3, bf16[128,256]{1,0:T(8,128)(2,1)} %c_ref.3, f32[128,16]{1,0:T(8,128)} %copy-done, f32[16,128]{1,0:T(8,128)} %bitcast.12, f32[128,16]{1,0:T(8,128)} %copy.18.dt_ref, ...), custom_call_target="tpu_custom_call" | custom-call | tf_op jit(solution)/shard_map/pallas_call | solution.py:515
  143.3 0.0 copy-start.3
  143.3 0.0 copy-start.6
  143.3 0.0 copy-start.5
  143.4 0.0 copy-done.2
  143.4 1.0 copy.26
  144.3 0.0 copy-done.1
  144.3 1.0 copy.27
  145.3 0.0 copy-done.4
  145.3 0.7 copy.28
  146.0 0.0 copy-done.3
  146.0 1.0 copy.29
  146.9 0.0 copy-done.6
  146.9 0.7 copy.30
  147.6 0.0 copy-done.5
  147.6 0.7 copy.31
  (1 shorter events, 0.0 us)
Async XLA Ops:
  1.7 2.8 %copy-start = (f32[128,16]{1,0:T(8,128)}, f32[128,16]{1,0:T(8,128)S(1)}, u32[]{:S(2)}) copy-start(f32[128,16]{1,0:T(8,128)S(1)} %reduce_window_sum.11.cum_ref) | copy-start | bytes 24580
  108.1 35.3 %copy-start.2 = (f32[128,2048]{1,0:T(8,128)S(1)}, f32[128,2048]{1,0:T(8,128)}, u32[]{:S(2)}) copy-start(f32[128,2048]{1,0:T(8,128)} %get-tuple-element.34) | copy-start | bytes 3145732
  108.1 36.3 %copy-start.1 = (f32[128,2048]{1,0:T(8,128)S(1)}, f32[128,2048]{1,0:T(8,128)}, u32[]{:S(2)}) copy-start(f32[128,2048]{1,0:T(8,128)} %get-tuple-element.35) | copy-start | bytes 3145732
  108.1 37.2 %copy-start.4 = (f32[128,256]{1,0:T(8,128)S(1)}, f32[128,256]{1,0:T(8,128)}, u32[]{:S(2)}) copy-start(f32[128,256]{1,0:T(8,128)} %get-tuple-element.36) | copy-start | bytes 393220
  143.3 2.6 %copy-start.3 = (f32[128,2048]{1,0:T(8,128)S(1)}, f32[128,2048]{1,0:T(8,128)}, u32[]{:S(2)}) copy-start(f32[128,2048]{1,0:T(8,128)} %get-tuple-element.37) | copy-start | bytes 3145732
  143.3 3.6 %copy-start.6 = (f32[128,256]{1,0:T(8,128)S(1)}, f32[128,256]{1,0:T(8,128)}, u32[]{:S(2)}) copy-start(f32[128,256]{1,0:T(8,128)} %get-tuple-element.38) | copy-start | bytes 393220
  143.3 4.3 %copy-start.5 = (f32[128,256]{1,0:T(8,128)S(1)}, f32[128,256]{1,0:T(8,128)}, u32[]{:S(2)}) copy-start(f32[128,256]{1,0:T(8,128)} %get-tuple-element.39) | copy-start | bytes 393220

commit v2 on v1

--- a/solution.py
+++ b/solution.py
@@ -96,10 +96,10 @@
 
 def forward_kernel(
     ctx_count, sizes,
-    x_ref, b_ref, c_ref, cum_ref, cumt_ref, dt_ref, dtt_ref, skip_ref, dec_ref, w_ref, k_ref,
+    x_ref, b_ref, c_ref, cum_ref, cumt_ref, dt_ref, dtt_ref, skip_ref, dec_ref, w_hbm, k_ref,
     kall_out, vall_out, ent_out, decall_out,
     kall, vall, decall, st_send, st_recv, en_send, en_recv, y_acc, y_b, vp_send, vp_recv,
-    st_s, st_r, en_s, en_r, k_s, k_r, v_s, v_r, d_s, d_r, p_s, p_r,
+    st_s, st_r, en_s, en_r, k_s, k_r, v_s, v_r, d_s, d_r, p_s, p_r, w_ref, w_s,
 ):
     me = lax.axis_index("ctx")
     mine = group_place(sizes)
@@ -108,6 +108,8 @@
     heads = x_ref.shape[1] // LANE
     per_group = heads // (b_ref.shape[1] // LANE)
     rows = heads * LANE // ctx_count
+    load = pltpu.make_async_copy(w_hbm, w_ref, w_s)
+    load.start()
     kall[...] = jnp.zeros_like(kall)
     vall[...] = jnp.zeros_like(vall)
     enter(ctx_count, sizes)
@@ -190,6 +192,7 @@
         carried = nn(c_ref[:, group * LANE:(group + 1) * LANE], en_recv[span, :])
         y_b[:, span] = rounded(y_acc[:, span] + jnp.exp(cum_ref[:, head:head + 1]) * carried)
     kv = k_ref.shape[1]
+    load.wait()
     for hop in list(range(1, members)) + [0]:
         place = lax.rem(mine + hop, members)
         piece = nn(y_b[...], w_ref[:, pl.ds(pl.multiple_of(place * kv, LANE), kv)])
@@ -243,7 +246,7 @@
     ctx_count, sizes,
     q_ref, do_ref, kall_ref, vall_ref,
     o_ref, dq_ref, dk_ref, vg_out,
-    k_flip, v_flip, s_buf, dp_buf, dk_acc, dv_acc, g_send, g_recv, vg_all,
+    k_flip, v_flip, q_cat, do_cat, q_t, do_t, o_t, dq_t, s_buf, dk_acc, dv_acc, g_send, g_recv, vg_all,
     g_s, g_r, vg_s, vg_r,
 ):
     me = lax.axis_index("ctx")
@@ -255,81 +258,62 @@
     chunk = math.gcd(seq, 256)
     chunks = (me * tok + tok - 1) // chunk + 1
     scale_by = 1.0 / math.sqrt(LANE)
-    pair = 2 * LANE
-    cols = 2 * tok
+    cols = REP * tok
     g_recv[...] = jnp.zeros_like(g_recv)
-    dk_acc[...] = jnp.zeros_like(dk_acc)
-    dv_acc[...] = jnp.zeros_like(dv_acc)
     enter(ctx_count, sizes)
     query_pos = me * tok + lax.rem(lax.broadcasted_iota(jnp.int32, (chunk, cols), 1), tok)
     key_pos = lax.broadcasted_iota(jnp.int32, (chunk, cols), 0)
 
     for kv in range(kv_dev):
         span = slice(kv * LANE, (kv + 1) * LANE)
-
-        def flip_chunk(at, carry):
+        spans = [slice((kv * REP + at) * LANE, (kv * REP + at + 1) * LANE) for at in range(REP)]
+        for at, here in enumerate(spans):
+            there = slice(at * tok, (at + 1) * tok)
+            q_cat[there, :] = q_ref[:, here]
+            do_cat[there, :] = do_ref[:, here]
+            q_t[:, there] = flip(q_ref[:, here])
+            do_t[:, there] = flip(do_ref[:, here])
+        o_t[...] = jnp.zeros_like(o_t)
+        dq_t[...] = jnp.zeros_like(dq_t)
+
+        def scores(at, running):
+            top, total = running
             here = pl.ds(pl.multiple_of(at * chunk, LANE), chunk)
             k_flip[:, here] = flip(kall_ref[here, span])
             v_flip[:, here] = flip(vall_ref[here, span])
+            s = nn(kall_ref[here, span], q_t[...]) * scale_by
+            s = jnp.where(key_pos + at * chunk <= query_pos, s, NEG_FILL)
+            s_buf[here, :] = s
+            new_top = jnp.maximum(top, jnp.max(s, axis=0, keepdims=True))
+            block = jnp.sum(jnp.exp(s - new_top), axis=0, keepdims=True)
+            return (new_top, total * jnp.exp(top - new_top) + block)
+
+        top, total = lax.fori_loop(
+            0, chunks, scores, (jnp.full((1, cols), NEG_FILL, F32), jnp.zeros((1, cols), F32))
+        )
+        inverse = 1.0 / total
+
+        def outputs(at, carry):
+            here = pl.ds(pl.multiple_of(at * chunk, LANE), chunk)
+            p = jnp.exp(s_buf[here, :] - top) * inverse
+            s_buf[here, :] = p
+            p_b = rounded(p)
+            dv_acc[here, span] = nn(p_b, do_cat[...])
+            o_t[...] += nn(v_flip[:, here], p_b)
             return carry
 
-        lax.fori_loop(0, chunks, flip_chunk, 0)
-
-        def one_pair(index, carry):
-            first = pl.multiple_of(kv * REP * LANE + index * pair, pair)
-            second = pl.multiple_of(first + LANE, LANE)
-            q = jnp.concatenate([q_ref[:, pl.ds(first, LANE)], q_ref[:, pl.ds(second, LANE)]], axis=0)
-            do = jnp.concatenate(
-                [do_ref[:, pl.ds(first, LANE)], do_ref[:, pl.ds(second, LANE)]], axis=0
-            )
-            q_t = flip(q)
-            do_f = do.astype(F32).T
-            do_t = do_f.astype(BF16)
-
-            def scores(at, top):
-                here = pl.ds(pl.multiple_of(at * chunk, LANE), chunk)
-                s = nn(kall_ref[here, span], q_t) * scale_by
-                s = jnp.where(key_pos + at * chunk <= query_pos, s, NEG_FILL)
-                s_buf[here, :] = s
-                return jnp.maximum(top, jnp.max(s, axis=0, keepdims=True))
-
-            top = lax.fori_loop(0, chunks, scores, jnp.full((1, cols), NEG_FILL, F32))
-
-            def totals(at, total):
-                here = pl.ds(pl.multiple_of(at * chunk, LANE), chunk)
-                e = jnp.exp(s_buf[here, :] - top)
-                s_buf[here, :] = e
-                dp_buf[here, :] = nn(vall_ref[here, span], do_t)
-                return total + jnp.sum(e, axis=0, keepdims=True)
-
-            total = lax.fori_loop(0, chunks, totals, jnp.zeros((1, cols), F32))
-            inverse = 1.0 / total
-
-            def outputs(at, o_t):
-                here = pl.ds(pl.multiple_of(at * chunk, LANE), chunk)
-                p = s_buf[here, :] * inverse
-                s_buf[here, :] = p
-                p_b = rounded(p)
-                dv_acc[here, span] += nn(p_b, do)
-                return o_t + nn(v_flip[:, here], p_b)
-
-            o_t = lax.fori_loop(0, chunks, outputs, jnp.zeros((LANE, cols), F32))
-            delta = jnp.sum(o_t * do_f, axis=0, keepdims=True)
-
-            def grads(at, dq_t):
-                here = pl.ds(pl.multiple_of(at * chunk, LANE), chunk)
-                ds = rounded(s_buf[here, :] * (dp_buf[here, :] - delta))
-                dk_acc[here, span] += nn(ds, q)
-                return dq_t + nn(k_flip[:, here], ds)
-
-            dq_t = lax.fori_loop(0, chunks, grads, jnp.zeros((LANE, cols), F32)) * scale_by
-            o_ref[:, pl.ds(first, LANE)] = o_t[:, :tok].T
-            o_ref[:, pl.ds(second, LANE)] = o_t[:, tok:].T
-            dq_ref[:, pl.ds(first, LANE)] = dq_t[:, :tok].T
-            dq_ref[:, pl.ds(second, LANE)] = dq_t[:, tok:].T
+        lax.fori_loop(0, chunks, outputs, 0)
+        delta = jnp.sum(o_t[...] * do_t[...].astype(F32), axis=0, keepdims=True)
+
+        def grads(at, carry):
+            here = pl.ds(pl.multiple_of(at * chunk, LANE), chunk)
+            dprobs = nn(vall_ref[here, span], do_t[...])
+            ds = rounded(s_buf[here, :] * (dprobs - delta))
+            dk_acc[here, span] = nn(ds, q_cat[...])
+            dq_t[...] += nn(k_flip[:, here], ds)
             return carry
 
-        lax.fori_loop(0, REP // 2, one_pair, 0)
+        lax.fori_loop(0, chunks, grads, 0)
         for hop in range(1, ctx_count):
             peer = ctx_peer(me, hop, ctx_count)
 
@@ -343,6 +327,10 @@
                     {"ctx": peer},
                 ).start()
 
+        for at, here in enumerate(spans):
+            there = slice(at * tok, (at + 1) * tok)
+            o_ref[:, here] = o_t[:, there].T
+            dq_ref[:, here] = dq_t[:, there].T * scale_by
     own = pl.ds(pl.multiple_of(me * tok, tok), tok)
     for kv in range(kv_dev):
         span = slice(kv * LANE, (kv + 1) * LANE)
@@ -392,10 +380,10 @@
 
 def backward_kernel(
     ctx_count,
-    x_ref, b_ref, c_ref, cum_ref, cumt_ref, dt_ref, dtt_ref, skip_ref, w_ref, ent_ref, decall, vg_ref,
+    x_ref, b_ref, c_ref, cum_ref, cumt_ref, dt_ref, dtt_ref, skip_ref, w_hbm, ent_ref, decall, vg_ref,
     dx_ref, db_ref, dc_ref,
     g_acc, st_send, st_recv, en_send, en_recv,
-    st_s, st_r, en_s, en_r,
+    st_s, st_r, en_s, en_r, w_ref, w_s,
 ):
     me = lax.axis_index("ctx")
     tok = x_ref.shape[0]
@@ -404,7 +392,10 @@
     per_group = heads // groups
     rows = heads * LANE // ctx_count
     kv = vg_ref.shape[2]
+    load = pltpu.make_async_copy(w_hbm, w_ref, w_s)
+    load.start()
     enter_ctx(ctx_count)
+    load.wait()
     for group in range(groups):
         wide = slice(group * per_group * LANE, (group + 1) * per_group * LANE)
         total = None
@@ -511,11 +502,15 @@
     vmem = pl.BlockSpec(memory_space=pltpu.VMEM)
     dma = pltpu.SemaphoreType.DMA
 
+    weight_slot = [pltpu.VMEM(value_weight.shape, BF16), dma]
+
     def call(kernel, operands, outs, scratch, ident):
         return pl.pallas_call(
             kernel,
             out_shape=[jax.ShapeDtypeStruct(shape, kind) for shape, kind in outs],
-            in_specs=[vmem] * len(operands),
+            in_specs=[
+                pl.BlockSpec(memory_space=pl.ANY) if a is value_weight else vmem for a in operands
+            ],
             out_specs=[vmem] * len(outs),
             scratch_shapes=scratch,
             compiler_params=pltpu.CompilerParams(
@@ -540,7 +535,7 @@
             pltpu.VMEM((tok, heads * LANE), BF16),
             pltpu.VMEM((members, tok, kv), BF16),
             pltpu.VMEM((members, tok, kv), BF16),
-        ] + [dma((n,))] * 10 + [dma((members,))] * 2,
+        ] + [dma((n,))] * 10 + [dma((members,))] * 2 + weight_slot,
         0,
     )
     attn_out, grad_q, grad_k, vg = call(
@@ -550,8 +545,13 @@
         [
             pltpu.VMEM((LANE, seq), BF16),
             pltpu.VMEM((LANE, seq), BF16),
-            pltpu.VMEM((seq, 2 * tok), F32),
-            pltpu.VMEM((seq, 2 * tok), F32),
+            pltpu.VMEM((REP * tok, LANE), BF16),
+            pltpu.VMEM((REP * tok, LANE), BF16),
+            pltpu.VMEM((LANE, REP * tok), BF16),
+            pltpu.VMEM((LANE, REP * tok), BF16),
+            pltpu.VMEM((LANE, REP * tok), F32),
+            pltpu.VMEM((LANE, REP * tok), F32),
+            pltpu.VMEM((seq, REP * tok), F32),
             pltpu.VMEM((seq, kv), F32),
             pltpu.VMEM((seq, kv), F32),
             pltpu.VMEM((kv_dev, n, 2, tok, LANE), BF16),
@@ -571,7 +571,7 @@
             pltpu.VMEM((n, rows, LANE), BF16),
             pltpu.VMEM((n, rows, LANE), BF16),
             pltpu.VMEM((heads * LANE, LANE), BF16),
-        ] + [dma((n,))] * 4,
+        ] + [dma((n,))] * 4 + weight_slot,
         2,
     )
     return (attn_out, grad_q, grad_k, grad_x, grad_b, grad_c)

time: 151 us -> 138 us (0.914)
  Pallas kernels: 139 us -> 127 us
    pallas_call x3, Pallas kernels: 139 us -> 127 us  [call(): pl.pallas_call(kernel, out_shape=[jax.ShapeDtypeStruct(shape, kind) for s...]
where the time goes in v2:
time: 138 us; the launch traced here: 136 us
  Pallas kernels  127 us (92%)
  local copies, waits for them, and re-layouts  7.78 us (6%)
    pallas_call x3, Pallas kernels, call(): pl.pallas_call(kernel, out_shape=[jax.ShapeDtypeStruct(shape, kind) for s...  127 us
    unnamed x21, local copies, waits for them, and re-layouts  6.33 us

profile of v2, /device:TPU:0, one launch (start us, length us, event | category | flops | bytes accessed | tf_op | source)
XLA Modules:
  0.0 136.2 jit_solution(8453365864231438951)
XLA Ops:
  0.6 0.8 negate_multiply_fusion
  1.4 0.1 copy.16
  1.5 0.2 reduce_window_sum.11.cum_ref
  1.7 0.0 copy-start
  1.7 0.7 broadcast_in_dim.5.dec_ref
  2.4 0.7 copy.17
  3.0 1.4 %copy.18.dt_ref = f32[128,16]{1,0:T(8,128)} copy(f32[128,16]{0,1:T(8,128)} %param.13) | data formatting | bytes 16384 | tf_op args[3]
  4.5 0.0 copy-done
  4.5 49.7 %shard_map.145 = (bf16[8,128,256]{2,1,0:T(8,128)(2,1)}, bf16[8,128,256]{2,1,0:T(8,128)(2,1)}, bf16[2048,128]{1,0:T(8,128)(2,1)}, f32[8,16,128]{2,1,0:T(8,128)}) custom-call(bf16[128,2048]{1,0:T(8,128)(2,1)} %x_ref.3, bf16[128,256]{1,0:T(8,128)(2,1)} %b_ref.3, bf16[128,256]{1,0:T(8,128)(2,1)} %c_ref.3, f32[128,16]{1,0:T(8,128)} %copy-done, ...), custom_call_target="tpu_custom_call" | custom-call | tf_op jit(solution)/shard_map/pallas_call | solution.py:508
  54.2 44.5 %shard_map.146 = (f32[128,2048]{1,0:T(8,128)}, f32[128,2048]{1,0:T(8,128)}, f32[128,256]{1,0:T(8,128)}, bf16[4,128,256]{2,1,0:T(8,128)(2,1)}) custom-call(bf16[128,2048]{1,0:T(8,128)(2,1)} %q_ref.1, bf16[128,2048]{1,0:T(8,128)(2,1)} %do_ref.1, bf16[1024,256]{1,0:T(8,128)(2,1)} %bitcast.7, bf16[1024,256]{1,0:T(8,128)(2,1)} %bitcast.8), custom_call_target="tpu_custom_call" | custom-call | tf_op jit(solution)/shard_map/pallas_call | solution.py:508
  98.8 0.0 copy-start.2
  98.8 0.0 copy-start.1
  98.8 0.0 copy-start.4
  98.8 32.5 %shard_map.147 = (f32[128,2048]{1,0:T(8,128)}, f32[128,256]{1,0:T(8,128)}, f32[128,256]{1,0:T(8,128)}) custom-call(bf16[128,2048]{1,0:T(8,128)(2,1)} %x_ref.3, bf16[128,256]{1,0:T(8,128)(2,1)} %b_ref.3, bf16[128,256]{1,0:T(8,128)(2,1)} %c_ref.3, f32[128,16]{1,0:T(8,128)} %copy-done, f32[16,128]{1,0:T(8,128)} %bitcast.12, f32[128,16]{1,0:T(8,128)} %copy.18.dt_ref, ...), custom_call_target="tpu_custom_call" | custom-call | tf_op jit(solution)/shard_map/pallas_call | solution.py:508
  131.3 0.0 copy-start.3
  131.3 0.0 copy-start.6
  131.3 0.0 copy-start.5
  131.3 0.0 copy-done.2
  131.3 1.0 copy.26
  132.3 0.0 copy-done.1
  132.3 1.0 copy.27
  133.2 0.0 copy-done.4
  133.2 0.7 copy.28
  133.9 0.0 copy-done.3
  133.9 1.0 copy.29
  134.9 0.0 copy-done.6
  134.9 0.7 copy.30
  135.5 0.0 copy-done.5
  135.5 0.7 copy.31
  (1 shorter events, 0.0 us)
Async XLA Ops:
  1.7 2.8 %copy-start = (f32[128,16]{1,0:T(8,128)}, f32[128,16]{1,0:T(8,128)S(1)}, u32[]{:S(2)}) copy-start(f32[128,16]{1,0:T(8,128)S(1)} %reduce_window_sum.11.cum_ref) | copy-start | bytes 24580
  98.8 32.5 %copy-start.2 = (f32[128,2048]{1,0:T(8,128)S(1)}, f32[128,2048]{1,0:T(8,128)}, u32[]{:S(2)}) copy-start(f32[128,2048]{1,0:T(8,128)} %get-tuple-element.34) | copy-start | bytes 3145732
  98.8 33.5 %copy-start.1 = (f32[128,2048]{1,0:T(8,128)S(1)}, f32[128,2048]{1,0:T(8,128)}, u32[]{:S(2)}) copy-start(f32[128,2048]{1,0:T(8,128)} %get-tuple-element.35) | copy-start | bytes 3145732
  98.8 34.5 %copy-start.4 = (f32[128,256]{1,0:T(8,128)S(1)}, f32[128,256]{1,0:T(8,128)}, u32[]{:S(2)}) copy-start(f32[128,256]{1,0:T(8,128)} %get-tuple-element.36) | copy-start | bytes 393220
  131.3 2.6 %copy-start.3 = (f32[128,2048]{1,0:T(8,128)S(1)}, f32[128,2048]{1,0:T(8,128)}, u32[]{:S(2)}) copy-start(f32[128,2048]{1,0:T(8,128)} %get-tuple-element.37) | copy-start | bytes 3145732
  131.3 3.6 %copy-start.6 = (f32[128,256]{1,0:T(8,128)S(1)}, f32[128,256]{1,0:T(8,128)}, u32[]{:S(2)}) copy-start(f32[128,256]{1,0:T(8,128)} %get-tuple-element.38) | copy-start | bytes 393220
  131.3 4.3 %copy-start.5 = (f32[128,256]{1,0:T(8,128)S(1)}, f32[128,256]{1,0:T(8,128)}, u32[]{:S(2)}) copy-start(f32[128,256]{1,0:T(8,128)} %get-tuple-element.39) | copy-start | bytes 393220

commit v3 on v2

--- a/solution.py
+++ b/solution.py
@@ -35,6 +35,10 @@
     return a.astype(BF16)
 
 
+def half_peer(me, hop, span):
+    return me // span * span + lax.rem(me + hop, span)
+
+
 def ctx_peer(me, hop, count):
     return lax.rem(me + hop, count)
 
@@ -99,7 +103,7 @@
     x_ref, b_ref, c_ref, cum_ref, cumt_ref, dt_ref, dtt_ref, skip_ref, dec_ref, w_hbm, k_ref,
     kall_out, vall_out, ent_out, decall_out,
     kall, vall, decall, st_send, st_recv, en_send, en_recv, y_acc, y_b, vp_send, vp_recv,
-    st_s, st_r, en_s, en_r, k_s, k_r, v_s, v_r, d_s, d_r, p_s, p_r, w_ref, w_s,
+    st_s, st_r, en_s, en_r, k_s, k_r, v_s, v_r, d_s, d_r, p_s, p_r, w_ref, w_s, ca_send, ca_recv, ca_s, ca_r,
 ):
     me = lax.axis_index("ctx")
     mine = group_place(sizes)
@@ -107,11 +111,16 @@
     tok = x_ref.shape[0]
     heads = x_ref.shape[1] // LANE
     per_group = heads // (b_ref.shape[1] // LANE)
-    rows = heads * LANE // ctx_count
+    span_count = ctx_count // 2
+    low = lax.rem(me, span_count)
+    other = {"ctx": ctx_peer(me, span_count, ctx_count)}
+    rows = heads * LANE // span_count
+    ca_recv[...] = jnp.zeros_like(ca_recv)
     load = pltpu.make_async_copy(w_hbm, w_ref, w_s)
     load.start()
     kall[...] = jnp.zeros_like(kall)
     vall[...] = jnp.zeros_like(vall)
+    decall[...] = jnp.zeros_like(decall)
     enter(ctx_count, sizes)
     decall[me] = dec_ref[...]
     kall[me] = k_ref[...]
@@ -124,24 +133,17 @@
         xw = x_ref[:, head * LANE:(head + 1) * LANE].astype(F32) * weight
         st_send[head * LANE:(head + 1) * LANE, :] = rounded(nn(b_flip, rounded(xw)))
     sends = []
-    for hop in range(1, ctx_count):
-        peer = ctx_peer(me, hop, ctx_count)
+    for hop in range(1, span_count):
+        peer = half_peer(me, hop, span_count)
         to = {"ctx": peer}
         copy = remote(decall.at[me], decall.at[me], d_s.at[hop], d_r.at[hop], to)
         copy.start()
         sends.append(copy)
-        block = pl.ds(pl.multiple_of(peer * rows, 16), rows)
-        copy = remote(st_send.at[block], st_recv.at[me], st_s.at[hop], st_r.at[hop], to)
+        block = pl.ds(pl.multiple_of(lax.rem(peer, span_count) * rows, 16), rows)
+        copy = remote(st_send.at[block], st_recv.at[low], st_s.at[hop], st_r.at[hop], to)
         copy.start()
         sends.append(copy)
-    for hop in range(1, ctx_count):
-        peer = ctx_peer(me, hop, ctx_count)
-
-        @pl.when(peer > me)
-        def _():
-            remote(kall.at[me], kall.at[me], k_s.at[hop], k_r.at[hop], {"ctx": peer}).start()
-
-    st_recv[me] = st_send[pl.ds(pl.multiple_of(me * rows, 16), rows), :]
+    st_recv[low] = st_send[pl.ds(pl.multiple_of(low * rows, 16), rows), :]
     lower = triangle(tok, True)
     for head in range(heads):
         group = head // per_group
@@ -152,37 +154,55 @@
         decays = jnp.where(lower, jnp.exp(jnp.where(lower, gap, 0.0)), 0.0)
         mixing = inner * decays * dtt_ref[head:head + 1, :]
         high = rounded(mixing)
-        low = rounded(mixing - high.astype(F32))
+        rest = rounded(mixing - high.astype(F32))
         x_head = x_ref[:, head * LANE:(head + 1) * LANE]
         y_acc[:, head * LANE:(head + 1) * LANE] = (
-            nn(high, x_head) + nn(low, x_head) + skip_ref[:, head:head + 1] * x_head.astype(F32)
-        )
-    for hop in range(1, ctx_count):
-        peer = ctx_peer(me, ctx_count - hop, ctx_count)
+            nn(high, x_head) + nn(rest, x_head) + skip_ref[:, head:head + 1] * x_head.astype(F32)
+        )
+    for hop in range(1, span_count):
+        peer = half_peer(me, span_count - hop, span_count)
         to = {"ctx": peer}
         remote(decall.at[me], decall.at[peer], d_s.at[hop], d_r.at[hop], to).wait_recv()
         remote(
-            st_send.at[pl.ds(0, rows)], st_recv.at[peer], st_s.at[hop], st_r.at[hop], to
+            st_send.at[pl.ds(0, rows)], st_recv.at[lax.rem(peer, span_count)], st_s.at[hop], st_r.at[hop], to
         ).wait_recv()
-    running = [jnp.zeros((part.stop - part.start, LANE), F32) for part, _ in scan_parts(me, rows)]
-    for block in range(ctx_count):
-        for at, (part, head) in enumerate(scan_parts(me, rows)):
+    @pl.when(me >= span_count)
+    def _():
+        remote(ca_send, ca_recv, ca_s, ca_r, other).wait_recv()
+
+    running = [ca_recv[part, :].astype(F32) for part, _ in scan_parts(low, rows)]
+    for block in range(span_count):
+        for at, (part, head) in enumerate(scan_parts(low, rows)):
             en_send[block, part, :] = rounded(running[at])
             running[at] = (
-                decall[block, pl.ds(head, 1), :] * running[at] + st_recv[block, part, :].astype(F32)
+                decall[me // span_count * span_count + block, pl.ds(head, 1), :] * running[at] + st_recv[block, part, :].astype(F32)
             )
-    own_rows = pl.ds(pl.multiple_of(me * rows, 16), rows)
+    for at, (part, _) in enumerate(scan_parts(low, rows)):
+        ca_send[part, :] = rounded(running[at])
+
+    @pl.when(me < span_count)
+    def _():
+        remote(ca_send, ca_recv, ca_s, ca_r, other).start()
+
+    own_rows = pl.ds(pl.multiple_of(low * rows, 16), rows)
+    for hop in range(1, span_count):
+        peer = half_peer(me, hop, span_count)
+        copy = remote(
+            en_send.at[lax.rem(peer, span_count)], en_recv.at[own_rows], en_s.at[hop], en_r.at[hop], {"ctx": peer}
+        )
+        copy.start()
+        sends.append(copy)
     for hop in range(1, ctx_count):
         peer = ctx_peer(me, hop, ctx_count)
-        copy = remote(
-            en_send.at[peer], en_recv.at[own_rows], en_s.at[hop], en_r.at[hop], {"ctx": peer}
-        )
-        copy.start()
-        sends.append(copy)
-    en_recv[own_rows, :] = en_send[me]
-    for hop in range(1, ctx_count):
-        peer = ctx_peer(me, ctx_count - hop, ctx_count)
-        block = pl.ds(pl.multiple_of(peer * rows, 16), rows)
+
+        @pl.when(peer > me)
+        def _():
+            remote(kall.at[me], kall.at[me], k_s.at[hop], k_r.at[hop], {"ctx": peer}).start()
+
+    en_recv[own_rows, :] = en_send[low]
+    for hop in range(1, span_count):
+        peer = half_peer(me, span_count - hop, span_count)
+        block = pl.ds(pl.multiple_of(lax.rem(peer, span_count) * rows, 16), rows)
         remote(
             en_send.at[0], en_recv.at[block], en_s.at[hop], en_r.at[hop], {"ctx": peer}
         ).wait_recv()
@@ -232,6 +252,11 @@
     decall_out[...] = decall[...]
     for copy in sends:
         copy.wait_send()
+
+    @pl.when(me < span_count)
+    def _():
+        remote(ca_send, ca_recv, ca_s, ca_r, other).wait_send()
+
     for hop in range(1, ctx_count):
         peer = ctx_peer(me, hop, ctx_count)
 
@@ -383,14 +408,18 @@
     x_ref, b_ref, c_ref, cum_ref, cumt_ref, dt_ref, dtt_ref, skip_ref, w_hbm, ent_ref, decall, vg_ref,
     dx_ref, db_ref, dc_ref,
     g_acc, st_send, st_recv, en_send, en_recv,
-    st_s, st_r, en_s, en_r, w_ref, w_s,
+    st_s, st_r, en_s, en_r, w_ref, w_s, ca_send, ca_recv, ca_s, ca_r,
 ):
     me = lax.axis_index("ctx")
     tok = x_ref.shape[0]
     heads = x_ref.shape[1] // LANE
     groups = b_ref.shape[1] // LANE
     per_group = heads // groups
-    rows = heads * LANE // ctx_count
+    span_count = ctx_count // 2
+    low = lax.rem(me, span_count)
+    other = {"ctx": ctx_peer(me, span_count, ctx_count)}
+    rows = heads * LANE // span_count
+    ca_recv[...] = jnp.zeros_like(ca_recv)
     kv = vg_ref.shape[2]
     load = pltpu.make_async_copy(w_hbm, w_ref, w_s)
     load.start()
@@ -409,14 +438,14 @@
             scaled = rounded(jnp.exp(cum_ref[:, head:head + 1]) * g_acc[:, span])
             st_send[span, :] = rounded(nn(c_flip, scaled))
     sends = []
-    for hop in range(1, ctx_count):
-        peer = ctx_peer(me, hop, ctx_count)
-        block = pl.ds(pl.multiple_of(peer * rows, 16), rows)
-        copy = remote(st_send.at[block], st_recv.at[me], st_s.at[hop], st_r.at[hop], {"ctx": peer})
+    for hop in range(1, span_count):
+        peer = half_peer(me, hop, span_count)
+        block = pl.ds(pl.multiple_of(lax.rem(peer, span_count) * rows, 16), rows)
+        copy = remote(st_send.at[block], st_recv.at[low], st_s.at[hop], st_r.at[hop], {"ctx": peer})
         copy.start()
         sends.append(copy)
-    own_rows = pl.ds(pl.multiple_of(me * rows, 16), rows)
-    st_recv[me] = st_send[own_rows, :]
+    own_rows = pl.ds(pl.multiple_of(low * rows, 16), rows)
+    st_recv[low] = st_send[own_rows, :]
     lower = triangle(tok, True)
     upper = triangle(tok, False)
     for group in range(groups):
@@ -440,29 +469,40 @@
             dc = dc + nt(rounded(jnp.exp(cum) * g), ent_ref[span, :])
         dc_ref[:, columns] = dc + nn(rounded(inner_grad), b)
         db_ref[:, columns] = nn(rounded(inner_grad.T), c)
-    for hop in range(1, ctx_count):
-        peer = ctx_peer(me, ctx_count - hop, ctx_count)
+    for hop in range(1, span_count):
+        peer = half_peer(me, span_count - hop, span_count)
         remote(
-            st_send.at[pl.ds(0, rows)], st_recv.at[peer], st_s.at[hop], st_r.at[hop], {"ctx": peer}
+            st_send.at[pl.ds(0, rows)], st_recv.at[lax.rem(peer, span_count)], st_s.at[hop], st_r.at[hop], {"ctx": peer}
         ).wait_recv()
-    running = [jnp.zeros((part.stop - part.start, LANE), F32) for part, _ in scan_parts(me, rows)]
-    for block in range(ctx_count - 1, -1, -1):
-        for at, (part, head) in enumerate(scan_parts(me, rows)):
+    @pl.when(me < span_count)
+    def _():
+        remote(ca_send, ca_recv, ca_s, ca_r, other).wait_recv()
+
+    running = [ca_recv[part, :].astype(F32) for part, _ in scan_parts(low, rows)]
+    for block in range(span_count - 1, -1, -1):
+        for at, (part, head) in enumerate(scan_parts(low, rows)):
             en_send[block, part, :] = rounded(running[at])
             running[at] = (
-                decall[block, pl.ds(head, 1), :] * running[at] + st_recv[block, part, :].astype(F32)
+                decall[me // span_count * span_count + block, pl.ds(head, 1), :] * running[at] + st_recv[block, part, :].astype(F32)
             )
-    for hop in range(1, ctx_count):
-        peer = ctx_peer(me, hop, ctx_count)
+    for at, (part, _) in enumerate(scan_parts(low, rows)):
+        ca_send[part, :] = rounded(running[at])
+
+    @pl.when(me >= span_count)
+    def _():
+        remote(ca_send, ca_recv, ca_s, ca_r, other).start()
+
+    for hop in range(1, span_count):
+        peer = half_peer(me, hop, span_count)
         copy = remote(
-            en_send.at[peer], en_recv.at[own_rows], en_s.at[hop], en_r.at[hop], {"ctx": peer}
+            en_send.at[lax.rem(peer, span_count)], en_recv.at[own_rows], en_s.at[hop], en_r.at[hop], {"ctx": peer}
         )
         copy.start()
         sends.append(copy)
-    en_recv[own_rows, :] = en_send[me]
-    for hop in range(1, ctx_count):
-        peer = ctx_peer(me, ctx_count - hop, ctx_count)
-        block = pl.ds(pl.multiple_of(peer * rows, 16), rows)
+    en_recv[own_rows, :] = en_send[low]
+    for hop in range(1, span_count):
+        peer = half_peer(me, span_count - hop, span_count)
+        block = pl.ds(pl.multiple_of(lax.rem(peer, span_count) * rows, 16), rows)
         remote(
             en_send.at[0], en_recv.at[block], en_s.at[hop], en_r.at[hop], {"ctx": peer}
         ).wait_recv()
@@ -481,6 +521,10 @@
     for copy in sends:
         copy.wait_send()
 
+    @pl.when(me >= span_count)
+    def _():
+        remote(ca_send, ca_recv, ca_s, ca_r, other).wait_send()
+
 
 def body(
     sizes,
@@ -493,7 +537,8 @@
     kv = keys.shape[1]
     kv_dev = kv // LANE
     seq = n * tok
-    rows = heads * LANE // n
+    half = n // 2
+    rows = heads * LANE // half
     cum = jnp.cumsum(-step_dt * decay_a[None, :], axis=0)
     cum_t = cum.T
     dt_t = step_dt.T
@@ -502,7 +547,10 @@
     vmem = pl.BlockSpec(memory_space=pltpu.VMEM)
     dma = pltpu.SemaphoreType.DMA
 
-    weight_slot = [pltpu.VMEM(value_weight.shape, BF16), dma]
+    weight_slot = [
+        pltpu.VMEM(value_weight.shape, BF16), dma,
+        pltpu.VMEM((rows, LANE), BF16), pltpu.VMEM((rows, LANE), BF16), dma, dma,
+    ]
 
     def call(kernel, operands, outs, scratch, ident):
         return pl.pallas_call(
@@ -528,8 +576,8 @@
             pltpu.VMEM((n, tok, kv), BF16),
             pltpu.VMEM((n, heads, LANE), F32),
             pltpu.VMEM((heads * LANE, LANE), BF16),
-            pltpu.VMEM((n, rows, LANE), BF16),
-            pltpu.VMEM((n, rows, LANE), BF16),
+            pltpu.VMEM((half, rows, LANE), BF16),
+            pltpu.VMEM((half, rows, LANE), BF16),
             pltpu.VMEM((heads * LANE, LANE), BF16),
             pltpu.VMEM((tok, heads * LANE), F32),
             pltpu.VMEM((tok, heads * LANE), BF16),
@@ -568,8 +616,8 @@
         [
             pltpu.VMEM((tok, heads * LANE), F32),
             pltpu.VMEM((heads * LANE, LANE), BF16),
-            pltpu.VMEM((n, rows, LANE), BF16),
-            pltpu.VMEM((n, rows, LANE), BF16),
+            pltpu.VMEM((half, rows, LANE), BF16),
+            pltpu.VMEM((half, rows, LANE), BF16),
             pltpu.VMEM((heads * LANE, LANE), BF16),
         ] + [dma((n,))] * 4 + weight_slot,
         2,

time: 138 us -> 126 us (0.913); the launches traced: 136 us -> 126 us
  Pallas kernels: 127 us -> 116 us
    pallas_call x3, Pallas kernels: 127 us -> 116 us  [call(): pl.pallas_call(kernel, out_shape=[jax.ShapeDtypeStruct(shape, kind) for s...]
where the time goes in v3:
time: 126 us
  Pallas kernels  116 us (92%)
  local copies, waits for them, and re-layouts  7.78 us (6%)
    pallas_call x3, Pallas kernels, call(): pl.pallas_call(kernel, out_shape=[jax.ShapeDtypeStruct(shape, kind) for s...  116 us
    unnamed x21, local copies, waits for them, and re-layouts  6.33 us

profile of v3, /device:TPU:0, one launch (start us, length us, event | category | flops | bytes accessed | tf_op | source)
XLA Modules:
  0.0 125.7 jit_solution(10421675908235096593)
XLA Ops:
  0.6 0.8 negate_multiply_fusion
  1.4 0.1 copy.16
  1.5 0.2 reduce_window_sum.11.cum_ref
  1.7 0.0 copy-start
  1.7 0.7 broadcast_in_dim.5.dec_ref
  2.4 0.7 copy.17
  3.0 1.4 %copy.18.dt_ref = f32[128,16]{1,0:T(8,128)} copy(f32[128,16]{0,1:T(8,128)} %param.13) | data formatting | bytes 16384 | tf_op args[3]
  4.5 0.0 copy-done
  4.5 42.8 %shard_map.145 = (bf16[8,128,256]{2,1,0:T(8,128)(2,1)}, bf16[8,128,256]{2,1,0:T(8,128)(2,1)}, bf16[2048,128]{1,0:T(8,128)(2,1)}, f32[8,16,128]{2,1,0:T(8,128)}) custom-call(bf16[128,2048]{1,0:T(8,128)(2,1)} %x_ref.3, bf16[128,256]{1,0:T(8,128)(2,1)} %b_ref.3, bf16[128,256]{1,0:T(8,128)(2,1)} %c_ref.3, f32[128,16]{1,0:T(8,128)} %copy-done, ...), custom_call_target="tpu_custom_call" | custom-call | tf_op jit(solution)/shard_map/pallas_call | solution.py:556
  47.3 40.4 %shard_map.146 = (f32[128,2048]{1,0:T(8,128)}, f32[128,2048]{1,0:T(8,128)}, f32[128,256]{1,0:T(8,128)}, bf16[4,128,256]{2,1,0:T(8,128)(2,1)}) custom-call(bf16[128,2048]{1,0:T(8,128)(2,1)} %q_ref.1, bf16[128,2048]{1,0:T(8,128)(2,1)} %do_ref.1, bf16[1024,256]{1,0:T(8,128)(2,1)} %bitcast.7, bf16[1024,256]{1,0:T(8,128)(2,1)} %bitcast.8), custom_call_target="tpu_custom_call" | custom-call | tf_op jit(solution)/shard_map/pallas_call | solution.py:556
  87.7 0.0 copy-start.2
  87.7 0.0 copy-start.1
  87.7 0.0 copy-start.4
  87.7 33.0 %shard_map.147 = (f32[128,2048]{1,0:T(8,128)}, f32[128,256]{1,0:T(8,128)}, f32[128,256]{1,0:T(8,128)}) custom-call(bf16[128,2048]{1,0:T(8,128)(2,1)} %x_ref.3, bf16[128,256]{1,0:T(8,128)(2,1)} %b_ref.3, bf16[128,256]{1,0:T(8,128)(2,1)} %c_ref.3, f32[128,16]{1,0:T(8,128)} %copy-done, f32[16,128]{1,0:T(8,128)} %bitcast.12, f32[128,16]{1,0:T(8,128)} %copy.18.dt_ref, ...), custom_call_target="tpu_custom_call" | custom-call | tf_op jit(solution)/shard_map/pallas_call | solution.py:556
  120.7 0.0 copy-start.3
  120.7 0.0 copy-start.6
  120.8 0.0 copy-start.5
  120.8 0.0 copy-done.2
  120.8 1.0 copy.26
  121.8 0.0 copy-done.1
  121.8 1.0 copy.27
  122.7 0.0 copy-done.4
  122.7 0.7 copy.28
  123.4 0.0 copy-done.3
  123.4 1.0 copy.29
  124.4 0.0 copy-done.6
  124.4 0.7 copy.30
  125.0 0.0 copy-done.5
  125.0 0.7 copy.31
  (1 shorter events, 0.0 us)
Async XLA Ops:
  1.7 2.8 %copy-start = (f32[128,16]{1,0:T(8,128)}, f32[128,16]{1,0:T(8,128)S(1)}, u32[]{:S(2)}) copy-start(f32[128,16]{1,0:T(8,128)S(1)} %reduce_window_sum.11.cum_ref) | copy-start | bytes 24580
  87.7 33.1 %copy-start.2 = (f32[128,2048]{1,0:T(8,128)S(1)}, f32[128,2048]{1,0:T(8,128)}, u32[]{:S(2)}) copy-start(f32[128,2048]{1,0:T(8,128)} %get-tuple-element.34) | copy-start | bytes 3145732
  87.7 34.0 %copy-start.1 = (f32[128,2048]{1,0:T(8,128)S(1)}, f32[128,2048]{1,0:T(8,128)}, u32[]{:S(2)}) copy-start(f32[128,2048]{1,0:T(8,128)} %get-tuple-element.35) | copy-start | bytes 3145732
  87.7 35.0 %copy-start.4 = (f32[128,256]{1,0:T(8,128)S(1)}, f32[128,256]{1,0:T(8,128)}, u32[]{:S(2)}) copy-start(f32[128,256]{1,0:T(8,128)} %get-tuple-element.36) | copy-start | bytes 393220
  120.7 2.6 %copy-start.3 = (f32[128,2048]{1,0:T(8,128)S(1)}, f32[128,2048]{1,0:T(8,128)}, u32[]{:S(2)}) copy-start(f32[128,2048]{1,0:T(8,128)} %get-tuple-element.37) | copy-start | bytes 3145732
  120.7 3.6 %copy-start.6 = (f32[128,256]{1,0:T(8,128)S(1)}, f32[128,256]{1,0:T(8,128)}, u32[]{:S(2)}) copy-start(f32[128,256]{1,0:T(8,128)} %get-tuple-element.38) | copy-start | bytes 393220
  120.8 4.3 %copy-start.5 = (f32[128,256]{1,0:T(8,128)S(1)}, f32[128,256]{1,0:T(8,128)}, u32[]{:S(2)}) copy-start(f32[128,256]{1,0:T(8,128)} %get-tuple-element.39) | copy-start | bytes 393220
